TPU v7x, 32 devices: a whole 2x2x4 slice. The times are simulated.
32 devices in a mesh: ctx: 8 (over z, x), rep: 4 (over y, core).
Axes of the slice: x: 2, y: 2, z: 4, core: 2. Of those that a mesh axis runs over, the one named last changes fastest.
Arguments:
- query: bfloat16 [4096, 2048], P(('rep', 'ctx')), parts along dimension 0, may hold values from -6 to 6
- key: bfloat16 [4096, 2048], P(('rep', 'ctx')), parts along dimension 0, may hold values from -6 to 6
- value: bfloat16 [4096, 2048], P(('rep', 'ctx')), parts along dimension 0, may hold values from -6 to 6
- beta: float32 [4096, 16], P(('rep', 'ctx')), parts along dimension 0, may hold values from 0.05 to 0.95
- log_gate: float32 [4096, 16], P(('rep', 'ctx')), parts along dimension 0, may hold values from -1.5 to 0
- level_weight: float32 [4096, 16, 4], P(('rep', 'ctx')), parts along dimension 0, may hold values from 0.1 to 1.5
- norm_gain: float32 [128], replicated, may hold values from 0.5 to 1.5
- grad_out: bfloat16 [4096, 2048], P(('rep', 'ctx')), parts along dimension 0, may hold values from -6 to 6
- grad_final_state: float32 [8192, 128], P(('rep', 'ctx')), parts along dimension 0, may hold values from -6 to 6
Outputs:
- grad_query: bfloat16 [4096, 2048], P(('rep', 'ctx')), parts along dimension 0
- grad_key: bfloat16 [4096, 2048], P(('rep', 'ctx')), parts along dimension 0
- grad_value: bfloat16 [4096, 2048], P(('rep', 'ctx')), parts along dimension 0
- grad_beta: float32 [4096, 16], P(('rep', 'ctx')), parts along dimension 0
- grad_level: float32 [4096, 16, 4], P(('rep', 'ctx')), parts along dimension 0
- grad_gain: float32 [512], P('rep'), parts along dimension 0
- final_state: float32 [8192, 128], P(('rep', 'ctx')), parts along dimension 0
There are 4 independent parts, one for each index of `rep`. A program takes and returns all parts, laid end to end along the dimension named above; an argument that names none is the same for every part. Nothing has to cross between parts.
All inputs are finite; a program needn't handle non-finite values.
Results may differ from a plain program's by a relative error of at most 0.001.
Values sent between devices are 32-bit elements; how exact they have to be, the bound alone decides.
A program may use at most 128 MiB of HBM per device.

v0:
```python
import jax
import jax.numpy as jnp
from jax import lax
from jax.sharding import PartitionSpec as P

epsilon = 1e-06
topmost_level = lax.Precision.HIGHEST


def from_partner(value, axis, bit):
    mask = 2**bit
    pairs = [(source, source ^ mask) for source in range(lax.axis_size(axis))]
    return lax.ppermute(value, axis, pairs)


def normalize(values):
    return values * lax.rsqrt(jnp.sum(values * values, axis=-1, keepdims=True) + epsilon)


def split_heads(values, head_count):
    row_count = values.shape[0]
    return values.reshape(row_count, head_count, -1).transpose(1, 0, 2)


def prepare(query, key, value, beta, cum_gate):
    head_count = cum_gate.shape[0]
    row_count = cum_gate.shape[1]
    query_normed = normalize(split_heads(query, head_count))
    normalized_key = normalize(split_heads(key, head_count))
    value_heads = split_heads(value, head_count)
    beta_heads = beta.T
    strict = jnp.tril(jnp.ones((row_count, row_count), dtype=bool), -1)
    log_gaps = cum_gate[:, :, None] - cum_gate[:, None, :]
    decays = jnp.exp(jnp.where(strict[None], log_gaps, -jnp.inf))
    key_inner = jnp.einsum("htk,hsk->hts", normalized_key, normalized_key, precision=topmost_level)
    system = (
        jnp.eye(row_count, dtype=cum_gate.dtype)[None] + beta_heads[:, :, None] * decays * key_inner
    )
    surrogate_value = jax.scipy.linalg.solve_triangular(
        system, beta_heads[:, :, None] * value_heads, lower=True
    )
    trailing_decay = jnp.exp(cum_gate[:, -1:] - cum_gate)
    state_per_block = jnp.einsum(
        "fni,fnb->fib",
        normalized_key * trailing_decay[:, :, None],
        surrogate_value,
        precision=topmost_level,
    )
    return (query_normed, normalized_key, surrogate_value, state_per_block)


def finish(
    query_normed, normalized_key, surrogate_value, level_weight, norm_gain, bucket_states, cum_gate
):
    row_count = cum_gate.shape[1]
    inclusive = jnp.tril(jnp.ones((row_count, row_count), dtype=bool))
    log_gaps = cum_gate[:, :, None] - cum_gate[:, None, :]
    decays = jnp.exp(jnp.where(inclusive[None], log_gaps, -jnp.inf))
    attention_scores = (
        jnp.einsum("htk,hsk->hts", query_normed, normalized_key, precision=topmost_level) * decays
    )
    intra_out = jnp.einsum(
        "hts,hsv->htv", attention_scores, surrogate_value, precision=topmost_level
    )
    cross_out = jnp.einsum("htk,lhkv->lhtv", query_normed, bucket_states, precision=topmost_level)
    level_heads = level_weight.transpose(1, 0, 2)
    weighted = level_heads[:, :, 1:] * jnp.exp(cum_gate)[:, :, None]
    mixture = level_heads[:, :, 0:1] * intra_out + jnp.einsum(
        "htl,lhtv->htv", weighted, cross_out, precision=topmost_level
    )
    inverse_rms = lax.rsqrt(jnp.mean(mixture * mixture, axis=-1, keepdims=True) + epsilon)
    normed = mixture * inverse_rms * norm_gain
    return normed.transpose(1, 0, 2).reshape(row_count, -1)


def local(query, key, value, beta, log_gate, level_weight, norm_gain, grad_out, grad_final_state):
    levels = level_weight.shape[2]
    cum_gate = jnp.cumsum(log_gate.T, axis=1)
    block_grand_total = cum_gate[:, -1]

    def local_prepare(query_float, key_float, value_float, beta_float):
        return prepare(query_float, key_float, value_float, beta_float, cum_gate)

    prepared, prepare_back = jax.vjp(
        local_prepare,
        query.astype(jnp.float32),
        key.astype(jnp.float32),
        value.astype(jnp.float32),
        beta,
    )
    query_normed, normalized_key, surrogate_value, state_per_block = prepared
    device = lax.axis_index("ctx")
    aggregate = state_per_block
    group_total = block_grand_total
    offset = jnp.zeros_like(block_grand_total)
    records = []
    bucket_list = []
    for degree in range(levels - 1):
        is_upper = device >> degree & 1 == 1
        if degree < levels - 2:
            partner, partner_total = from_partner((aggregate, group_total), "ctx", degree)
        else:
            partner, partner_total = from_partner((aggregate, group_total), "ctx", degree)
        bucket_list.append(jnp.where(is_upper, jnp.exp(offset)[:, None, None] * partner, 0.0))
        records.append((is_upper, offset, group_total, partner_total))
        aggregate = jnp.where(
            is_upper,
            jnp.exp(group_total)[:, None, None] * partner + aggregate,
            jnp.exp(partner_total)[:, None, None] * aggregate + partner,
        )
        offset = jnp.where(is_upper, offset + partner_total, offset)
        group_total = group_total + partner_total
    bucket_stack = jnp.stack(bucket_list)
    rows_dev = grad_final_state.shape[0]
    rows_total = aggregate.shape[0] * aggregate.shape[1]
    full_rows = aggregate.reshape(rows_total, -1)
    own_rows = lax.dynamic_slice_in_dim(full_rows, device * rows_dev, rows_dev, 0)

    def local_finish(normed_queries, normed_keys, pseudo_rows, level_rows, gain_rows, bucket_rows):
        return finish(
            normed_queries, normed_keys, pseudo_rows, level_rows, gain_rows, bucket_rows, cum_gate
        )

    mixed_out, finish_back = jax.vjp(
        local_finish,
        query_normed,
        normalized_key,
        surrogate_value,
        level_weight,
        norm_gain,
        bucket_stack,
    )
    grad_qnormed, grad_knormed, grad_pseudo, grad_level, grad_gain_local, grad_buckets = (
        finish_back(grad_out.astype(jnp.float32))
    )
    seed_rows = lax.dynamic_update_slice_in_dim(
        jnp.zeros((rows_total, grad_final_state.shape[1]), jnp.float32),
        grad_final_state,
        device * rows_dev,
        0,
    )
    adjoint = seed_rows.reshape(state_per_block.shape)
    for degree in reversed(range(levels - 1)):
        is_upper, offset, group_total, partner_total = records[degree]
        outgoing = jnp.where(
            is_upper,
            jnp.exp(offset)[:, None, None] * grad_buckets[degree]
            + jnp.exp(group_total)[:, None, None] * adjoint,
            adjoint,
        )
        retained = jnp.where(is_upper, adjoint, jnp.exp(partner_total)[:, None, None] * adjoint)
        incoming = from_partner(outgoing, "ctx", degree)
        adjoint = retained + incoming
    grad_query, grad_key, grad_value, grad_beta = prepare_back(
        (grad_qnormed, grad_knormed, grad_pseudo, adjoint)
    )
    grad_gain = lax.psum(grad_gain_local, "ctx")
    return (
        grad_query.astype(jnp.bfloat16),
        grad_key.astype(jnp.bfloat16),
        grad_value.astype(jnp.bfloat16),
        grad_beta,
        grad_level,
        grad_gain,
        own_rows,
    )


def solution(mesh):
    in_specs = (
        P(("rep", "ctx"), None),
        P(("rep", "ctx"), None),
        P(("rep", "ctx"), None),
        P(("rep", "ctx"), None),
        P(("rep", "ctx"), None),
        P(("rep", "ctx"), None, None),
        P(),
        P(("rep", "ctx"), None),
        P(("rep", "ctx"), None),
    )
    out_specs = (
        P(("rep", "ctx"), None),
        P(("rep", "ctx"), None),
        P(("rep", "ctx"), None),
        P(("rep", "ctx"), None),
        P(("rep", "ctx"), None, None),
        P("rep"),
        P(("rep", "ctx"), None),
    )
    return jax.shard_map(local, mesh=mesh, in_specs=in_specs, out_specs=out_specs, check_vma=False)
```

profile of v0, /device:TPU:0, one launch (start us, length us, event | category | flops | bytes accessed | tf_op | source)
XLA Modules:
  0.0 423.9 jit_solution(13142008598209138384)
XLA Ops:
  7.9 158.8 %custom-call.7 = f32[16,1,128,128]{2,3,1,0:T(8,128)} custom-call(f32[16,1,128,128]{3,2,1,0:T(8,128)} %fusion.26), custom_call_target="InvertDiagBlocksLowerTriangular" | custom-call | tf_op jit(solution)/shard_map/jvp(jit(_solve_triangular))/vmap()/triangular_solve | solution.py:39
  166.8 3.4 fusion.45
  171.4 3.0 collective-permute-start
  174.5 23.2 %collective-permute-done.1 = f32[16]{0:T(128)S(1)} collective-permute-done((f32[16]{0:T(128)S(1)}, f32[16]{0:T(128)S(1)}, u32[]{:S(2)}, u32[]{:S(2)}) %collective-permute-start.1) | collective-permute-done | bytes 96 | tf_op jit(solution)/shard_map/ppermute | solution.py:13
  201.2 2.5 select_bitcast_fusion.2
  205.5 21.4 %collective-permute-done.2 = f32[16,128,128]{2,1,0:T(8,128)S(1)} collective-permute-done((f32[16,128,128]{2,1,0:T(8,128)S(1)}, f32[16,128,128]{2,1,0:T(8,128)S(1)}, u32[]{:S(2)}, u32[]{:S(2)}) %collective-permute-start.2) | collective-permute-done | bytes 1048608 | tf_op jit(solution)/shard_map/ppermute | solution.py:13
  228.6 2.5 collective-permute-start.4
  234.3 3.0 convolution_multiply_fusion.1
  240.0 34.6 %collective-permute-done.5 = f32[16]{0:T(128)S(1)} collective-permute-done((f32[16]{0:T(128)S(1)}, f32[16]{0:T(128)S(1)}, u32[]{:S(2)}, u32[]{:S(2)}) %collective-permute-start.5) | collective-permute-done | bytes 96 | tf_op jit(solution)/shard_map/ppermute | solution.py:13
  274.6 2.9 add_select_fusion
  277.5 5.8 %fusion.1 = (f32[16,128,128]{1,2,0:T(8,128)S(1)}, f32[16,3,128,128]{3,2,1,0:T(8,128)S(1)}) fusion(f32[16,128,3]{1,2,0:T(4,128)S(1)} %slice_multiply_fusion, f32[16,128,128]{1,2,0:T(8,128)S(1)} %bitcast.187, f32[16,128]{1,0:T(8,128)S(1)} %add_rsqrt_fusion.1, f32[1,16,128,128]{3,2,1,0:T(8,128)S(1)} %get-tuple-element.35, ...), kind=kOutput, calls=%fused_computation.4 | convolution fusion | flops 1211105280 | bytes 8421376 | tf_op jit(solution)/shard_map/jvp(htk,lhkv->lhtv)/dot_general | solution.py:65
  287.0 4.0 fusion.8
  291.0 2.2 fusion.40
  295.3 45.7 %collective-permute-done.6 = f32[16,128,128]{2,1,0:T(8,128)S(1)} collective-permute-done((f32[16,128,128]{2,1,0:T(8,128)S(1)}, f32[16,128,128]{2,1,0:T(8,128)S(1)}, u32[]{:S(2)}, u32[]{:S(2)}) %collective-permute-start.6) | collective-permute-done | bytes 1048608 | tf_op jit(solution)/shard_map/ppermute | solution.py:13
  341.1 3.0 fusion.37
  344.0 2.4 fusion.69
  346.5 3.4 multiply_reduce_fusion.3
  352.9 28.4 %psum.7 = f32[128]{0:T(128)} all-reduce(f32[128]{0:T(128)S(1)} %get-tuple-element.22), channel_id=1, replica_groups=mesh['ctx'=8,'rep'=4] {'ctx'}, use_global_device_ids=true, to_apply=%region_11.13 | all-reduce | flops 128 | bytes 1024 | tf_op jit(solution)/shard_map/psum | solution.py:157
  381.3 2.8 fusion.34
  389.5 15.2 %collective-permute-done.8 = f32[16,128,128]{2,1,0:T(8,128)S(1)} collective-permute-done((f32[16,128,128]{2,1,0:T(8,128)S(1)}, f32[16,128,128]{2,1,0:T(8,128)S(1)}, u32[]{:S(2)}, u32[]{:S(2)}) %collective-permute-start.8) | collective-permute-done | bytes 1048608 | tf_op jit(solution)/shard_map/ppermute | solution.py:13
  406.7 2.3 fusion.119
  410.6 2.5 fusion.27
  414.7 2.6 fusion.103
  417.3 2.7 multiply_reduce_fusion.2
  (103 shorter events, 44.3 us)
Async XLA Ops:
  2.0 4.4 %copy-start.16 = (f32[128,16]{0,1:T(8,128)S(1)}, f32[128,16]{0,1:T(8,128)}, u32[]{:S(2)}) copy-start(f32[128,16]{0,1:T(8,128)} %param.14) | copy-start | bytes 24580
  2.2 164.6 %copy-start.8 = (f32[128,16,128]{2,0,1:T(8,128)}, f32[128,16,128]{2,0,1:T(8,128)S(1)}, u32[]{:S(2)}) copy-start(f32[128,16,128]{2,0,1:T(8,128)S(1)} %copy.56) | copy-start | bytes 3145732
  6.4 160.3 %copy-start.12 = (f32[16,128,128]{2,1,0:T(8,128)}, f32[16,128,128]{2,1,0:T(8,128)S(1)}, u32[]{:S(2)}) copy-start(f32[16,128,128]{2,1,0:T(8,128)S(1)} %fusion.72) | copy-start | bytes 3145732
  171.4 29.8 %collective-permute-start = (f32[16,128,128]{2,1,0:T(8,128)S(1)}, f32[16,128,128]{2,1,0:T(8,128)}, u32[]{:S(2)}, u32[]{:S(2)}) collective-permute-start(f32[16,128,128]{2,1,0:T(8,128)S(1)} %fusion.55), channel_id=1, source_target_pairs={{0,4},{4,0},{8,12},{12,8},{16,20},{20,16},{24,28},{28,24},{1,5},{5... | collective-permute-start | bytes 3145736 | tf_op jit(solution)/shard_map/ppermute | solution.py:13
  174.4 23.3 %collective-permute-start.1 = (f32[16]{0:T(128)S(1)}, f32[16]{0:T(128)S(1)}, u32[]{:S(2)}, u32[]{:S(2)}) collective-permute-start(f32[16]{0:T(128)S(1)} %slice_reduce_fusion), channel_id=1, source_target_pairs={{0,4},{4,0},{8,12},{12,8},{16,20},{20,16},{24,28},{28,24},{1,5},{5... | collective-permute-start | bytes 200 | tf_op jit(solution)/shard_map/ppermute | solution.py:13
  197.7 3.5 collective-permute-start.3
  203.7 28.7 %copy-start.18 = (f32[128,16,4]{0,2,1:T(4,128)S(1)}, f32[128,16,4]{0,2,1:T(4,128)}, u32[]{:S(2)}) copy-start(f32[128,16,4]{0,2,1:T(4,128)} %param.16) | copy-start | bytes 98308
  203.7 23.2 %collective-permute-start.2 = (f32[16,128,128]{2,1,0:T(8,128)S(1)}, f32[16,128,128]{2,1,0:T(8,128)S(1)}, u32[]{:S(2)}, u32[]{:S(2)}) collective-permute-start(f32[16,128,128]{2,1,0:T(8,128)S(1)} %get-tuple-element.41), channel_id=1, source_target_pairs={{0,8},{4,12},{8,0},{12,4},{16,24},{20,28},{24,16},{28,20},{1,9},{5... | collective-permute-start | bytes 3145736 | tf_op jit(solution)/shard_map/ppermute | solution.py:13
  226.9 6.6 %copy-start.17 = (f32[256,128]{1,0:T(8,128)S(1)}, f32[256,128]{1,0:T(8,128)}, u32[]{:S(2)}) copy-start(f32[256,128]{1,0:T(8,128)} %param.19) | copy-start | bytes 393220
  228.6 46.0 %collective-permute-start.4 = (f32[16,128,128]{2,1,0:T(8,128)}, f32[16,128,128]{2,1,0:T(8,128)}, u32[]{:S(2)}, u32[]{:S(2)}) collective-permute-start(f32[16,128,128]{2,1,0:T(8,128)} %get-tuple-element.43), channel_id=1, source_target_pairs={{0,16},{4,20},{8,24},{12,28},{16,0},{20,4},{24,8},{28,12},{1,17},{... | collective-permute-start | bytes 3145736 | tf_op jit(solution)/shard_map/ppermute | solution.py:13
  237.3 37.3 %collective-permute-start.5 = (f32[16]{0:T(128)S(1)}, f32[16]{0:T(128)S(1)}, u32[]{:S(2)}, u32[]{:S(2)}) collective-permute-start(f32[16]{0:T(128)S(1)} %get-tuple-element.29), channel_id=1, source_target_pairs={{0,16},{4,20},{8,24},{12,28},{16,0},{20,4},{24,8},{28,12},{1,17},{... | collective-permute-start | bytes 200 | tf_op jit(solution)/shard_map/ppermute | solution.py:13
  239.9 37.5 %copy-start.11 = (f32[1,16,128,128]{3,2,1,0:T(8,128)S(1)}, f32[1,16,128,128]{3,2,1,0:T(8,128)}, u32[]{:S(2)}) copy-start(f32[1,16,128,128]{3,2,1,0:T(8,128)} %get-tuple-element.40) | copy-start | bytes 3145732
  239.9 37.5 %copy-start.14 = (f32[1,16,128,128]{3,2,1,0:T(8,128)S(1)}, f32[1,16,128,128]{3,2,1,0:T(8,128)}, u32[]{:S(2)}) copy-start(f32[1,16,128,128]{3,2,1,0:T(8,128)} %get-tuple-element.42) | copy-start | bytes 3145732
  277.5 5.8 %copy-start.4 = (f32[16,128,128]{2,1,0:T(8,128)S(1)}, f32[16,128,128]{2,1,0:T(8,128)}, u32[]{:S(2)}) copy-start(f32[16,128,128]{2,1,0:T(8,128)} %convolution_multiply_fusion.1) | copy-start | bytes 3145732
  286.0 60.5 %copy-start = (f32[16,128,128]{1,2,0:T(8,128)}, f32[16,128,128]{1,2,0:T(8,128)S(1)}, u32[]{:S(2)}) copy-start(f32[16,128,128]{1,2,0:T(8,128)S(1)} %get-tuple-element.25) | copy-start | bytes 3145732
  291.0 50.1 %copy-start.3 = (f32[3,16,128,128]{3,2,1,0:T(8,128)}, f32[3,16,128,128]{3,2,1,0:T(8,128)S(1)}, u32[]{:S(2)}) copy-start(f32[3,16,128,128]{3,2,1,0:T(8,128)S(1)} %fusion.8) | copy-start | bytes 9437188
  293.2 47.8 %collective-permute-start.6 = (f32[16,128,128]{2,1,0:T(8,128)S(1)}, f32[16,128,128]{2,1,0:T(8,128)S(1)}, u32[]{:S(2)}, u32[]{:S(2)}) collective-permute-start(f32[16,128,128]{2,1,0:T(8,128)S(1)} %fusion.40), channel_id=1, source_target_pairs={{0,16},{4,20},{8,24},{12,28},{16,0},{20,4},{24,8},{28,12},{1,17},{... | collective-permute-start | bytes 3145736 | tf_op jit(solution)/shard_map/ppermute | solution.py:13
  295.3 51.1 %copy-start.6 = (f32[16,128,128]{2,1,0:T(8,128)}, f32[16,128,128]{2,1,0:T(8,128)S(1)}, u32[]{:S(2)}) copy-start(f32[16,128,128]{2,1,0:T(8,128)S(1)} %convolution_multiply_fusion) | copy-start | bytes 3145732
  344.0 37.3 %collective-permute-start.7 = (f32[16,128,128]{2,1,0:T(8,128)}, f32[16,128,128]{2,1,0:T(8,128)}, u32[]{:S(2)}, u32[]{:S(2)}) collective-permute-start(f32[16,128,128]{2,1,0:T(8,128)} %fusion.37), channel_id=1, source_target_pairs={{0,8},{4,12},{8,0},{12,4},{16,24},{20,28},{24,16},{28,20},{1,9},{5... | collective-permute-start | bytes 3145736 | tf_op jit(solution)/shard_map/ppermute | solution.py:13
  381.3 5.2 %copy-start.1 = (f32[16,128,128]{1,2,0:T(8,128)S(1)}, f32[16,128,128]{1,2,0:T(8,128)}, u32[]{:S(2)}) copy-start(f32[16,128,128]{1,2,0:T(8,128)} %copy-done) | copy-start | bytes 3145732
  381.3 5.2 %copy-start.5 = (f32[16,128,128]{2,1,0:T(8,128)S(1)}, f32[16,128,128]{2,1,0:T(8,128)}, u32[]{:S(2)}) copy-start(f32[16,128,128]{2,1,0:T(8,128)} %convolution_multiply_fusion.1) | copy-start | bytes 3145732
  384.2 20.5 %collective-permute-start.8 = (f32[16,128,128]{2,1,0:T(8,128)S(1)}, f32[16,128,128]{2,1,0:T(8,128)S(1)}, u32[]{:S(2)}, u32[]{:S(2)}) collective-permute-start(f32[16,128,128]{2,1,0:T(8,128)S(1)} %get-tuple-element.26), channel_id=1, source_target_pairs={{0,4},{4,0},{8,12},{12,8},{16,20},{20,16},{24,28},{28,24},{1,5},{5... | collective-permute-start | bytes 3145736 | tf_op jit(solution)/shard_map/ppermute | solution.py:13
  404.7 4.3 %copy-start.9 = (f32[128,16,128]{2,0,1:T(8,128)S(1)}, f32[128,16,128]{2,0,1:T(8,128)}, u32[]{:S(2)}) copy-start(f32[128,16,128]{2,0,1:T(8,128)} %copy-done.8) | copy-start | bytes 3145732
  404.7 4.3 %copy-start.10 = (f32[16,1,128,128]{2,3,1,0:T(8,128)S(1)}, f32[16,1,128,128]{2,3,1,0:T(8,128)}, u32[]{:S(2)}) copy-start(f32[16,1,128,128]{2,3,1,0:T(8,128)} %custom-call.7) | copy-start | bytes 3145732
  (6 other events, 18.4 us)
where the time goes:
time: 429 us; the launch traced here: 424 us
  other arithmetic  181 us (42%)
  waiting for transfers between devices  142 us (33%)
  matrix products  47.2 us (11%)
  blocking collectives  28.4 us (7%)
  local copies, waits for them, and re-layouts  14.5 us (3%)
  starting transfers between devices  9.81 us (2%)
    another operation x2, other arithmetic, prepare(): jax.scipy.linalg.solve_triangular(system, beta_heads[:, :, None] * value_...  160 us
    ppermute x9, waiting for transfers between devices, from_partner(): return lax.ppermute(value, axis, pairs)  142 us
    psum x1, blocking collectives, local(): grad_gain = lax.psum(grad_gain_local, 'ctx')  28.4 us
    dot_general x3, matrix products, finish(): jnp.einsum('htk,lhkv->lhtv', query_normed, bucket_states, precision=topmo...  13.1 us
    ppermute x9, starting transfers between devices, from_partner(): return lax.ppermute(value, axis, pairs)  9.81 us
  transfers between devices with their start and end apart: 9, of which 6 were waited for; matrix products, arithmetic and copies ran while one was open for 6% of the time, Pallas kernels for 0%

commit v1 on v0

v1 whole, which is shorter than its diff:
```python
import functools

import jax
import jax.numpy as jnp
from jax import lax
from jax.experimental import pallas as pl
from jax.experimental.pallas import tpu as pltpu
from jax.sharding import PartitionSpec as P

epsilon = 1e-06
topmost_level = lax.Precision.HIGHEST
NN = (((1,), (0,)), ((), ()))
NT = (((1,), (1,)), ((), ()))
CHUNKS = 4
HEADS_STEP = 2
VMEM_LIMIT = 48 * 2**20


def from_partner(value, axis, bit):
    mask = 2**bit
    pairs = [(source, source ^ mask) for source in range(lax.axis_size(axis))]
    return lax.ppermute(value, axis, pairs)


def cut(x):
    high = x.astype(jnp.bfloat16)
    return high, (x - high.astype(jnp.float32)).astype(jnp.bfloat16)


def dot1(a, b, dims=NN):
    return lax.dot_general(a, b, dims, preferred_element_type=jnp.float32)


def dot3(a, b, dims=NN):
    left = jnp.concatenate([a[0], a[1], a[0]], axis=1)
    right = jnp.concatenate([b[0], b[0], b[1]], axis=0 if dims is NN else 1)
    return dot1(left, right, dims)


def dot2_right(a, b, dims=NN):
    left = jnp.concatenate([a[0], a[1]], axis=1)
    right = jnp.concatenate([b, b], axis=0 if dims is NN else 1)
    return dot1(left, right, dims)


def dot2_left(a, b, dims=NN):
    left = jnp.concatenate([a, a], axis=1)
    right = jnp.concatenate([b[0], b[1]], axis=0 if dims is NN else 1)
    return dot1(left, right, dims)


def column(values, lane):
    lanes = lax.broadcasted_iota(jnp.int32, values.shape, 1)
    return jnp.sum(jnp.where(lanes == lane, values, 0.0), axis=1, keepdims=True)


def inverse_norm(values):
    return lax.rsqrt(jnp.sum(values * values, axis=-1, keepdims=True) + epsilon)


def coordinates(rows):
    shape = (rows, rows)
    return lax.broadcasted_iota(jnp.int32, shape, 0), lax.broadcasted_iota(jnp.int32, shape, 1)


def decay_of(gate_column, gate_row, keep):
    return jnp.exp(jnp.where(keep, gate_column - gate_row, -jnp.inf))


def prepare_kernel(base, k_ref, v_ref, beta_ref, cc_ref, cr_ref, t_ref, u_ref, s_ref):
    rows = k_ref.shape[0]
    width = t_ref.shape[2]
    size = s_ref.shape[1]
    t_ids, s_ids = coordinates(rows)
    systems = []
    for i in range(t_ref.shape[0]):
        head = base + pl.program_id(0) * t_ref.shape[0] + i
        key = k_ref[:, i * size : (i + 1) * size]
        gate = column(cc_ref[...], head)
        beta = column(beta_ref[...], head)
        gate_row = cr_ref[pl.ds(head, 1), :]
        key_float = key.astype(jnp.float32)
        key_normed = key_float * inverse_norm(key_float)
        keys = cut(key_normed)
        inner = dot3(keys, keys, NT)
        systems.append(
            beta * decay_of(gate, gate_row, s_ids < t_ids) * inner
        )
        systems[-1] = (systems[-1], gate, beta, key_normed)
    inverses = []
    for system, _, _, _ in systems:
        first = jnp.where((t_ids ^ s_ids) == 1, system, 0.0)
        inverses.append(jnp.where(t_ids == s_ids, 1.0, 0.0) - first)
    span = 2
    while span < rows:
        gap = t_ids ^ s_ids
        keep = (gap >= span) & (gap < 2 * span)
        for i, (system, _, _, _) in enumerate(systems):
            parts = cut(inverses[i])
            mixed = dot3(cut(jnp.where(keep, system, 0.0)), parts)
            inverses[i] = inverses[i] - dot3(parts, cut(mixed))
        span *= 2
    for i, (_, gate, beta, key_normed) in enumerate(systems):
        value = v_ref[:, i * u_ref.shape[2] : (i + 1) * u_ref.shape[2]].astype(jnp.float32)
        pseudo = dot3(cut(inverses[i]), cut(beta * value))
        trailing = jnp.exp(gate[rows - 1 :, :] - gate)
        state = dot3(cut((key_normed * trailing).T), cut(pseudo))
        t_ref[i] = inverses[i]
        u_ref[i] = pseudo
        s_ref[i] = state


def finish_kernel(
    base, levels, q_ref, k_ref, go_ref, u_ref, cc_ref, cr_ref, w_ref, f_ref, gain_ref, *refs
):
    bucket_refs = refs[: levels - 1]
    gq_ref, dk_ref, du_ref, gl_ref, gg_ref = refs[levels - 1 : levels + 4]
    back_refs = refs[levels + 4 :]
    rows = q_ref.shape[0]
    size = dk_ref.shape[2]
    vsize = du_ref.shape[2]
    heads = du_ref.shape[0]
    t_ids, s_ids = coordinates(rows)

    @pl.when(pl.program_id(0) == 0)
    def _():
        gl_ref[...] = jnp.zeros_like(gl_ref)
        gg_ref[...] = jnp.zeros_like(gg_ref)

    level_lanes = lax.broadcasted_iota(jnp.int32, gl_ref.shape, 1)
    grad_level = jnp.zeros(gl_ref.shape, jnp.float32)
    grad_gain = jnp.zeros(gg_ref.shape, jnp.float32)
    for i in range(heads):
        head = base + pl.program_id(0) * heads + i
        query = q_ref[:, i * size : (i + 1) * size]
        key = k_ref[:, i * size : (i + 1) * size]
        grad_out = go_ref[:, i * vsize : (i + 1) * vsize].astype(jnp.float32)
        gate = column(cc_ref[...], head)
        gate_row = cr_ref[pl.ds(head, 1), :]
        query_float = query.astype(jnp.float32)
        key_float = key.astype(jnp.float32)
        query_scale = inverse_norm(query_float)
        query_normed = query_float * query_scale
        key_normed = key_float * inverse_norm(key_float)
        queries = cut(query_normed)
        keys = cut(key_normed)
        pseudo = cut(u_ref[i])
        decay = decay_of(gate, gate_row, s_ids <= t_ids)
        scores = dot3(queries, keys, NT) * decay
        intra = dot3(cut(scores), pseudo)
        weight0 = column(w_ref[...], head * levels)
        mixture = weight0 * intra
        weights, crosses, buckets = [], [], []
        for l in range(levels - 1):
            bucket = cut(bucket_refs[l][i])
            cross = dot3(queries, bucket)
            weight = column(w_ref[...], head * levels + 1 + l)
            mixture = mixture + weight * cross
            weights.append(weight)
            crosses.append(cross)
            buckets.append(bucket)
        scale = lax.rsqrt(jnp.mean(mixture * mixture, axis=-1, keepdims=True) + epsilon)
        unit = mixture * scale
        grad_gain = grad_gain + jnp.sum(grad_out * unit, axis=0, keepdims=True)
        grad_unit = grad_out * gain_ref[...]
        grad_mix = scale * (
            grad_unit - unit * jnp.mean(grad_unit * unit, axis=-1, keepdims=True)
        )
        part = jnp.sum(grad_mix * intra, axis=-1, keepdims=True)
        grad_level = grad_level + jnp.where(level_lanes == head * levels, part, 0.0)
        grad_intra = weight0 * grad_mix
        grad_intra_parts = cut(grad_intra)
        grad_scores = dot3(grad_intra_parts, pseudo, NT) * decay
        grad_query = dot3(cut(grad_scores), keys)
        dk_ref[i] = dot3(cut(grad_scores.T), queries)
        du_ref[i] = dot3(cut(scores.T), grad_intra_parts)
        query_turned = cut(query_normed.T)
        for l in range(levels - 1):
            lane = head * levels + 1 + l
            part = jnp.sum(grad_mix * crosses[l], axis=-1, keepdims=True)
            part = part * column(f_ref[...], lane)
            grad_level = grad_level + jnp.where(level_lanes == lane, part, 0.0)
            weighted = cut(weights[l] * grad_mix)
            grad_query = grad_query + dot3(weighted, buckets[l], NT)
            back_refs[l][i] = dot3(query_turned, weighted)
        along = jnp.sum(grad_query * query_normed, axis=-1, keepdims=True)
        grad_query = query_scale * (grad_query - query_normed * along)
        gq_ref[:, i * size : (i + 1) * size] = grad_query.astype(gq_ref.dtype)
    gl_ref[...] += grad_level
    gg_ref[...] += grad_gain


def back_kernel(
    base, k_ref, v_ref, beta_ref, cc_ref, cr_ref, t_ref, u_ref, dk_ref, du_ref, ds_ref,
    gk_ref, gv_ref, gb_ref,
):
    rows = k_ref.shape[0]
    size = dk_ref.shape[2]
    vsize = du_ref.shape[2]
    heads = du_ref.shape[0]
    t_ids, s_ids = coordinates(rows)
    strict = s_ids < t_ids

    @pl.when(pl.program_id(0) == 0)
    def _():
        gb_ref[...] = jnp.zeros_like(gb_ref)

    lanes = lax.broadcasted_iota(jnp.int32, gb_ref.shape, 1)
    grad_beta = jnp.zeros(gb_ref.shape, jnp.float32)
    for i in range(heads):
        head = base + pl.program_id(0) * heads + i
        key_float = k_ref[:, i * size : (i + 1) * size].astype(jnp.float32)
        value = v_ref[:, i * vsize : (i + 1) * vsize].astype(jnp.float32)
        gate = column(cc_ref[...], head)
        beta = column(beta_ref[...], head)
        gate_row = cr_ref[pl.ds(head, 1), :]
        key_scale = inverse_norm(key_float)
        key_normed = key_float * key_scale
        keys = cut(key_normed)
        pseudo = cut(u_ref[i])
        state = cut(ds_ref[i])
        trailing = jnp.exp(gate[rows - 1 :, :] - gate)
        grad_pseudo = du_ref[i] + trailing * dot3(keys, state)
        grad_key = dk_ref[i] + trailing * dot3(pseudo, state, NT)
        solved = dot3(cut(t_ref[i].T), cut(grad_pseudo))
        solved_parts = cut(solved)
        decay = decay_of(gate, gate_row, strict)
        grad_system = -dot3(solved_parts, pseudo, NT) * decay
        inner = dot3(keys, keys, NT)
        part = jnp.sum(solved * value, axis=-1, keepdims=True) + jnp.sum(
            grad_system * inner, axis=-1, keepdims=True
        )
        grad_beta = grad_beta + jnp.where(lanes == head, part, 0.0)
        grad_inner = beta * grad_system
        grad_key = grad_key + dot3(cut(grad_inner + grad_inner.T), keys)
        along = jnp.sum(grad_key * key_normed, axis=-1, keepdims=True)
        grad_key = key_scale * (grad_key - key_normed * along)
        gk_ref[:, i * size : (i + 1) * size] = grad_key.astype(gk_ref.dtype)
        gv_ref[:, i * vsize : (i + 1) * vsize] = (beta * solved).astype(gv_ref.dtype)
    gb_ref[...] += grad_beta


def local(query, key, value, beta, log_gate, level_weight, norm_gain, grad_out, grad_final_state):
    rows, heads, levels = level_weight.shape
    size = query.shape[1] // heads
    vsize = value.shape[1] // heads
    chunks = CHUNKS if heads % (CHUNKS * HEADS_STEP) == 0 else 1
    per = heads // chunks
    step = HEADS_STEP if per % HEADS_STEP == 0 else 1
    steps = per // step
    device = lax.axis_index("ctx")
    blocks = lax.axis_size("ctx")

    lower = jnp.tril(jnp.ones((rows, rows), jnp.float32))
    gates = lax.dot_general(lower, log_gate, NN, precision=topmost_level)
    gates_row = gates.T
    totals = lax.all_gather(gates[-1], "ctx")
    ids = jnp.arange(blocks)
    degrees = levels - 1

    def group_sum(match):
        return jnp.sum(jnp.where(match[:, None], totals, 0.0), axis=0)

    offset = jnp.zeros((heads,), jnp.float32)
    uppers, offsets, own_sums, partner_sums = [], [], [], []
    for degree in range(degrees):
        own = ids >> degree == device >> degree
        other = ids >> degree == (device >> degree) ^ 1
        is_upper = device >> degree & 1 == 1
        uppers.append(is_upper)
        offsets.append(offset)
        own_sums.append(group_sum(own))
        partner_sums.append(group_sum(other))
        offset = jnp.where(is_upper, offset + partner_sums[-1], offset)
    factors = [jnp.ones((rows, heads), jnp.float32)]
    for degree in range(degrees):
        reach = jnp.where(uppers[degree], jnp.exp(offsets[degree]), 0.0)
        factors.append(jnp.exp(gates) * reach[None, :])
    factor = jnp.stack(factors, axis=2)
    weight = (level_weight * factor).reshape(rows, heads * levels)
    factor = factor.reshape(rows, heads * levels)

    def whole(array):
        return pl.BlockSpec(array.shape, lambda g: (0,) * array.ndim)

    def wide(chunk, width):
        return pl.BlockSpec((rows, step * width), lambda g: (0, chunk * steps + g))

    def tall(*dims):
        return pl.BlockSpec((step,) + dims, lambda g: (g, 0, 0))

    def fixed(*dims):
        return pl.BlockSpec(dims, lambda g: (0,) * len(dims))

    def floats(*dims):
        return jax.ShapeDtypeStruct(dims, jnp.float32)

    def call(kernel, name, in_specs, outs, out_specs, dots):
        return pl.pallas_call(
            kernel,
            name=name,
            grid=(steps,),
            in_specs=in_specs,
            out_specs=out_specs,
            out_shape=outs,
            compiler_params=pltpu.CompilerParams(vmem_limit_bytes=VMEM_LIMIT),
            cost_estimate=pl.CostEstimate(
                flops=per * dots * 6 * rows * rows * size * 4,
                bytes_accessed=per * rows * size * 4 * 8,
                transcendentals=per * rows * rows,
            ),
        )

    prepared = []
    for chunk in range(chunks):
        prepared.append(
            call(
                functools.partial(prepare_kernel, chunk * per),
                f"prepare{chunk}",
                [wide(chunk, size), wide(chunk, vsize), whole(beta), whole(gates), whole(gates_row)],
                (floats(per, rows, rows), floats(per, rows, vsize), floats(per, size, vsize)),
                (tall(rows, rows), tall(rows, vsize), tall(size, vsize)),
                16,
            )(key, value, beta, gates, gates_row)
        )

    def part_of(vector, chunk):
        return vector[chunk * per : (chunk + 1) * per][:, None, None]

    aggregates = [state for _, _, state in prepared]
    partners = [[None] * degrees for _ in range(chunks)]
    for degree in range(degrees):
        for chunk in range(chunks):
            partner = from_partner(aggregates[chunk], "ctx", degree)
            partners[chunk][degree] = partner
            upper = uppers[degree]
            own_factor = jnp.where(upper, 1.0, jnp.exp(partner_sums[degree]))
            other_factor = jnp.where(upper, jnp.exp(own_sums[degree]), 1.0)
            aggregates[chunk] = (
                part_of(own_factor, chunk) * aggregates[chunk]
                + part_of(other_factor, chunk) * partner
            )

    rows_dev = grad_final_state.shape[0]
    full_rows = jnp.concatenate(aggregates).reshape(heads * size, vsize)
    own_rows = lax.dynamic_slice_in_dim(full_rows, device * rows_dev, rows_dev, 0)
    seeds = lax.dynamic_update_slice_in_dim(
        jnp.zeros((heads * size, vsize), jnp.float32), grad_final_state, device * rows_dev, 0
    ).reshape(heads, size, vsize)

    gain = norm_gain[None, :]
    finished = []
    for chunk in range(chunks):
        _, pseudo, _ = prepared[chunk]
        finished.append(
            call(
                functools.partial(finish_kernel, chunk * per, levels),
                f"finish{chunk}",
                [wide(chunk, size), wide(chunk, size), wide(chunk, vsize), tall(rows, vsize)]
                + [whole(gates), whole(gates_row), whole(weight), whole(factor), whole(gain)]
                + [tall(size, vsize)] * degrees,
                (
                    jax.ShapeDtypeStruct((rows, per * size), jnp.bfloat16),
                    floats(per, rows, size),
                    floats(per, rows, vsize),
                    floats(rows, heads * levels),
                    floats(1, vsize),
                )
                + (floats(per, size, vsize),) * degrees,
                (
                    wide(0, size),
                    tall(rows, size),
                    tall(rows, vsize),
                    fixed(rows, heads * levels),
                    fixed(1, vsize),
                )
                + (tall(size, vsize),) * degrees,
                6 + 3 * degrees,
            )(
                query, key, grad_out, pseudo, gates, gates_row, weight, factor, gain,
                *partners[chunk],
            )
        )
    grad_gain = lax.psum(sum(result[4] for result in finished)[0], "ctx")

    adjoints = [seeds[chunk * per : (chunk + 1) * per] for chunk in range(chunks)]
    for degree in reversed(range(degrees)):
        for chunk in range(chunks):
            adjoint = adjoints[chunk]
            upper = uppers[degree]
            send_factor = jnp.where(upper, jnp.exp(own_sums[degree]), 1.0)
            keep_factor = jnp.where(upper, 1.0, jnp.exp(partner_sums[degree]))
            outgoing = finished[chunk][5 + degree] + part_of(send_factor, chunk) * adjoint
            incoming = from_partner(outgoing, "ctx", degree)
            adjoints[chunk] = part_of(keep_factor, chunk) * adjoint + incoming

    backs = []
    for chunk in range(chunks):
        inverse, pseudo, _ = prepared[chunk]
        grad_key, grad_pseudo = finished[chunk][1:3]
        backs.append(
            call(
                functools.partial(back_kernel, chunk * per),
                f"back{chunk}",
                [wide(chunk, size), wide(chunk, vsize), whole(beta), whole(gates), whole(gates_row)]
                + [tall(rows, rows), tall(rows, vsize), tall(rows, size), tall(rows, vsize)]
                + [tall(size, vsize)],
                (
                    jax.ShapeDtypeStruct((rows, per * size), jnp.bfloat16),
                    jax.ShapeDtypeStruct((rows, per * vsize), jnp.bfloat16),
                    floats(rows, heads),
                ),
                (wide(0, size), wide(0, vsize), fixed(rows, heads)),
                6,
            )(
                key, value, beta, gates, gates_row, inverse, pseudo, grad_key, grad_pseudo,
                adjoints[chunk],
            )
        )
    return (
        jnp.concatenate([result[0] for result in finished], axis=1),
        jnp.concatenate([result[0] for result in backs], axis=1),
        jnp.concatenate([result[1] for result in backs], axis=1),
        sum(result[2] for result in backs),
        sum(result[3] for result in finished).reshape(rows, heads, levels),
        grad_gain,
        own_rows,
    )


def solution(mesh):
    in_specs = (
        P(("rep", "ctx"), None),
        P(("rep", "ctx"), None),
        P(("rep", "ctx"), None),
        P(("rep", "ctx"), None),
        P(("rep", "ctx"), None),
        P(("rep", "ctx"), None, None),
        P(),
        P(("rep", "ctx"), None),
        P(("rep", "ctx"), None),
    )
    out_specs = (
        P(("rep", "ctx"), None),
        P(("rep", "ctx"), None),
        P(("rep", "ctx"), None),
        P(("rep", "ctx"), None),
        P(("rep", "ctx"), None, None),
        P("rep"),
        P(("rep", "ctx"), None),
    )
    return jax.shard_map(local, mesh=mesh, in_specs=in_specs, out_specs=out_specs, check_vma=False)
```

time: 429 us -> 221 us (0.52)
  other arithmetic: 181 us -> 18.3 us
  waiting for transfers between devices: 142 us -> 50.1 us
  Pallas kernels: 0 us -> 56 us
  matrix products: 47.2 us -> 0.18 us
  local copies, waits for them, and re-layouts: 14.5 us -> 31.2 us
  starting transfers between devices: 9.81 us -> 22.4 us
  blocking collectives: 28.4 us -> 40 us
    another operation x5 -> x2, other arithmetic: 165 us -> 0.15 us  [local(): factor = jnp.stack(factors, axis=2)]
    ppermute x9 -> x24, waiting for transfers between devices: 142 us -> 50.1 us  [from_partner(): return lax.ppermute(value, axis, pairs)]
    pallas_call x0 -> x12, Pallas kernels: none -> 56 us  [the longest x4 24.8 us: local(): call(functools.partial(prepare_kernel, chunk * per), f'prepare{chunk}', [...]
    dot_general x16 -> x1, matrix products: 39.8 us -> 0.18 us  [local(): gates = lax.dot_general(lower, log_gate, NN, precision=topmost_level)]
    all_gather x0 -> x1, blocking collectives: none -> 21.4 us  [local(): totals = lax.all_gather(gates[-1], 'ctx')]
    unnamed x46 -> x250, local copies, waits for them, and re-layouts: 5.46 us -> 24.7 us
    add x1 -> x26, other arithmetic: 0.01 us -> 13.9 us  [the longest x8 7.55 us: local(): finished[chunk][5 + degree] + part_of(send_factor, chunk) * adjoint]
    ppermute x9 -> x24, starting transfers between devices: 9.81 us -> 22.4 us  [from_partner(): return lax.ppermute(value, axis, pairs)]
  transfers between devices with their start and end apart: 9 -> 24, of which waited for: 6 -> 8; matrix products, arithmetic and copies ran while one was open for 6% -> 10% of each run, Pallas kernels for 0% -> 21%
where the time goes in v1:
time: 221 us; the launch traced here: 220 us
  Pallas kernels  56 us (25%)
  waiting for transfers between devices  50.1 us (23%)
  blocking collectives  40 us (18%)
  local copies, waits for them, and re-layouts  31.2 us (14%)
  starting transfers between devices  22.4 us (10%)
  other arithmetic  18.3 us (8%)
    ppermute x24, waiting for transfers between devices, from_partner(): return lax.ppermute(value, axis, pairs)  50.1 us
    pallas_call x4, Pallas kernels, local(): call(functools.partial(prepare_kernel, chunk * per), f'prepare{chunk}', [...  24.8 us
    unnamed x250, local copies, waits for them, and re-layouts  24.7 us
    ppermute x24, starting transfers between devices, from_partner(): return lax.ppermute(value, axis, pairs)  22.4 us
    all_gather x1, blocking collectives, local(): totals = lax.all_gather(gates[-1], 'ctx')  21.4 us
    pallas_call x4, Pallas kernels, local(): call(functools.partial(finish_kernel, chunk * per, levels), f'finish{chun...  19.5 us
    psum x1, blocking collectives, local(): grad_gain = lax.psum(sum((result[4] for result in finished))[0], 'ctx')  18.7 us
    pallas_call x4, Pallas kernels, local(): call(functools.partial(back_kernel, chunk * per), f'back{chunk}', [wide(c...  11.6 us
  transfers between devices with their start and end apart: 24, of which 8 were waited for; matrix products, arithmetic and copies ran while one was open for 10% of the time, Pallas kernels for 21%

profile of v1, /device:TPU:0, one launch (start us, length us, event | category | flops | bytes accessed | tf_op | source)
XLA Modules:
  0.0 220.0 jit_solution(3666362270113787773)
XLA Ops:
  4.5 6.2 %prepare0.1 = (f32[4,128,128]{2,1,0:T(8,128)S(1)}, f32[4,128,128]{2,1,0:T(8,128)S(1)}, f32[4,128,128]{2,1,0:T(8,128)S(1)}) custom-call(bf16[128,2048]{1,0:T(8,128)(2,1)S(1)} %copy-done.17, bf16[128,2048]{1,0:T(8,128)(2,1)S(1)} %copy-done.21, f32[128,16]{1,0:T(8,128)S(1)} %copy.74.beta_ref, f32[128,16]{1,0:T(8,128)S(1)} %copy.75.cc_ref, f32[16,128]{1,0:T(8,128)S(1)} %bitcast.22), custom_call_target="tpu_custom_call" | custom-call | flops 3221225472 | bytes 2097152 | tf_op jit(solution)/shard_map/prepare0/pallas_call | solution.py:317
  10.7 3.0 %collective-permute-start = (f32[4,128,128]{2,1,0:T(8,128)S(1)}, f32[4,128,128]{2,1,0:T(8,128)S(1)}, u32[]{:S(2)}, u32[]{:S(2)}) collective-permute-start(f32[4,128,128]{2,1,0:T(8,128)S(1)} %get-tuple-element.64), channel_id=1, source_target_pairs={{0,4},{4,0},{8,12},{12,8},{16,20},{20,16},{24,28},{28,24},{1,5},{5... | collective-permute-start | bytes 786440 | tf_op jit(solution)/shard_map/ppermute | solution.py:22
  13.7 6.2 %prepare1.1 = (f32[4,128,128]{2,1,0:T(8,128)S(1)}, f32[4,128,128]{2,1,0:T(8,128)S(1)}, f32[4,128,128]{2,1,0:T(8,128)S(1)}) custom-call(bf16[128,2048]{1,0:T(8,128)(2,1)S(1)} %copy-done.18, bf16[128,2048]{1,0:T(8,128)(2,1)S(1)} %copy-done.22, f32[128,16]{1,0:T(8,128)S(1)} %copy.74.beta_ref, f32[128,16]{1,0:T(8,128)S(1)} %copy.75.cc_ref, f32[16,128]{1,0:T(8,128)S(1)} %bitcast.23), custom_call_target="tpu_custom_call" | custom-call | flops 3221225472 | bytes 2097152 | tf_op jit(solution)/shard_map/prepare1/pallas_call | solution.py:317
  21.4 6.2 %prepare2.1 = (f32[4,128,128]{2,1,0:T(8,128)S(1)}, f32[4,128,128]{2,1,0:T(8,128)S(1)}, f32[4,128,128]{2,1,0:T(8,128)S(1)}) custom-call(bf16[128,2048]{1,0:T(8,128)(2,1)S(1)} %copy-done.18, bf16[128,2048]{1,0:T(8,128)(2,1)S(1)} %copy-done.22, f32[128,16]{1,0:T(8,128)S(1)} %copy.74.beta_ref, f32[128,16]{1,0:T(8,128)S(1)} %copy.75.cc_ref, f32[16,128]{1,0:T(8,128)S(1)} %bitcast.24), custom_call_target="tpu_custom_call" | custom-call | flops 3221225472 | bytes 2097152 | tf_op jit(solution)/shard_map/prepare2/pallas_call | solution.py:317
  31.1 6.2 %prepare3.1 = (f32[4,128,128]{2,1,0:T(8,128)S(1)}, f32[4,128,128]{2,1,0:T(8,128)S(1)}, f32[4,128,128]{2,1,0:T(8,128)S(1)}) custom-call(bf16[128,2048]{1,0:T(8,128)(2,1)S(1)} %copy-done.18, bf16[128,2048]{1,0:T(8,128)(2,1)S(1)} %copy-done.22, f32[128,16]{1,0:T(8,128)S(1)} %copy.74.beta_ref, f32[128,16]{1,0:T(8,128)S(1)} %copy.75.cc_ref, f32[16,128]{1,0:T(8,128)S(1)} %bitcast.25), custom_call_target="tpu_custom_call" | custom-call | flops 3221225472 | bytes 2097152 | tf_op jit(solution)/shard_map/prepare3/pallas_call | solution.py:317
  39.0 21.4 %all-gather = f32[8,1,16]{2,1,0:T(1,128)S(1)} all-gather(f32[1,1,16]{2,1,0:T(1,128)S(1)} %bitcast.55), channel_id=1, replica_groups=mesh['ctx'=8,'rep'=4] {'ctx'}, dimensions={0}, use_global_device_ids=true | all-gather | bytes 576 | tf_op jit(solution)/shard_map/all_gather | solution.py:257
  67.8 2.1 collective-permute-start.4
  71.4 2.1 collective-permute-start.10
  73.5 8.3 %collective-permute-done.1.refs_1_ = f32[4,128,128]{2,1,0:T(8,128)S(1)} collective-permute-done((f32[4,128,128]{2,1,0:T(8,128)S(1)}, f32[4,128,128]{2,1,0:T(8,128)S(1)}, u32[]{:S(2)}, u32[]{:S(2)}) %collective-permute-start.1) | collective-permute-done | bytes 262176 | tf_op jit(solution)/shard_map/ppermute | solution.py:22
  82.7 6.0 %collective-permute-done.4.refs_1_ = f32[4,128,128]{2,1,0:T(8,128)S(1)} collective-permute-done((f32[4,128,128]{2,1,0:T(8,128)S(1)}, f32[4,128,128]{2,1,0:T(8,128)S(1)}, u32[]{:S(2)}, u32[]{:S(2)}) %collective-permute-start.4) | collective-permute-done | bytes 262176 | tf_op jit(solution)/shard_map/ppermute | solution.py:22
  89.5 2.7 %collective-permute-done.7.refs_1_ = f32[4,128,128]{2,1,0:T(8,128)S(1)} collective-permute-done((f32[4,128,128]{2,1,0:T(8,128)S(1)}, f32[4,128,128]{2,1,0:T(8,128)S(1)}, u32[]{:S(2)}, u32[]{:S(2)}) %collective-permute-start.7) | collective-permute-done | bytes 262176 | tf_op jit(solution)/shard_map/ppermute | solution.py:22
  96.1 23.2 %collective-permute-done.2.refs_2_ = f32[4,128,128]{2,1,0:T(8,128)S(1)} collective-permute-done((f32[4,128,128]{2,1,0:T(8,128)S(1)}, f32[4,128,128]{2,1,0:T(8,128)S(1)}, u32[]{:S(2)}, u32[]{:S(2)}) %collective-permute-start.2) | collective-permute-done | bytes 262176 | tf_op jit(solution)/shard_map/ppermute | solution.py:22
  119.9 4.9 %finish0.1 = (bf16[128,512]{1,0:T(8,128)(2,1)S(1)}, f32[4,128,128]{2,1,0:T(8,128)S(1)}, f32[4,128,128]{2,1,0:T(8,128)S(1)}, f32[128,64]{1,0:T(8,128)S(1)}, f32[1...) custom-call(bf16[128,2048]{1,0:T(8,128)(2,1)S(1)} %copy-done.15, ...), custom_call_target="tpu_custom_call" | custom-call | flops 3019898880 | bytes 2097152 | tf_op jit(solution)/shard_map/finish0/pallas_call | solution.py:356
  126.4 4.9 %finish1.1 = (bf16[128,512]{1,0:T(8,128)(2,1)S(1)}, f32[4,128,128]{2,1,0:T(8,128)S(1)}, f32[4,128,128]{2,1,0:T(8,128)S(1)}, f32[128,64]{1,0:T(8,128)S(1)}, f32[1...) custom-call(bf16[128,2048]{1,0:T(8,128)(2,1)S(1)} %copy-done.15, ...), custom_call_target="tpu_custom_call" | custom-call | flops 3019898880 | bytes 2097152 | tf_op jit(solution)/shard_map/finish1/pallas_call | solution.py:356
  133.5 2.8 %collective-permute-start.15 = (f32[4,128,128]{2,1,0:T(8,128)}, f32[4,128,128]{2,1,0:T(8,128)}, u32[]{:S(2)}, u32[]{:S(2)}) collective-permute-start(f32[4,128,128]{2,1,0:T(8,128)} %multiply_add_fusion.20), channel_id=1, source_target_pairs={{0,16},{4,20},{8,24},{12,28},{16,0},{20,4},{24,8},{28,12},{1,17},{... | collective-permute-start | bytes 786440 | tf_op jit(solution)/shard_map/ppermute | solution.py:22
  136.3 4.9 %finish2.1 = (bf16[128,512]{1,0:T(8,128)(2,1)S(1)}, f32[4,128,128]{2,1,0:T(8,128)S(1)}, f32[4,128,128]{2,1,0:T(8,128)S(1)}, f32[128,64]{1,0:T(8,128)S(1)}, f32[1...) custom-call(bf16[128,2048]{1,0:T(8,128)(2,1)S(1)} %copy-done.15, ...), custom_call_target="tpu_custom_call" | custom-call | flops 3019898880 | bytes 2097152 | tf_op jit(solution)/shard_map/finish2/pallas_call | solution.py:356
  143.5 3.9 %collective-permute-done.11.refs_2_ = f32[4,128,128]{2,1,0:T(8,128)S(1)} collective-permute-done((f32[4,128,128]{2,1,0:T(8,128)S(1)}, f32[4,128,128]{2,1,0:T(8,128)S(1)}, u32[]{:S(2)}, u32[]{:S(2)}) %collective-permute-start.11) | collective-permute-done | bytes 262176 | tf_op jit(solution)/shard_map/ppermute | solution.py:22
  147.4 4.9 %finish3.1 = (bf16[128,512]{1,0:T(8,128)(2,1)S(1)}, f32[4,128,128]{2,1,0:T(8,128)S(1)}, f32[4,128,128]{2,1,0:T(8,128)S(1)}, f32[128,64]{1,0:T(8,128)S(1)}, f32[1...) custom-call(bf16[128,2048]{1,0:T(8,128)(2,1)S(1)} %copy-done.15, ...), custom_call_target="tpu_custom_call" | custom-call | flops 3019898880 | bytes 2097152 | tf_op jit(solution)/shard_map/finish3/pallas_call | solution.py:356
  156.6 18.7 %psum.7 = f32[128]{0:T(128)} all-reduce(f32[128]{0:T(128)} %add_bitcast_fusion), channel_id=1, replica_groups=mesh['ctx'=8,'rep'=4] {'ctx'}, use_global_device_ids=true, to_apply=%region_6.7 | all-reduce | flops 128 | bytes 1024 | tf_op jit(solution)/shard_map/psum | solution.py:384
  200.5 2.7 %collective-permute-done.20 = f32[4,128,128]{2,1,0:T(8,128)S(1)} collective-permute-done((f32[4,128,128]{2,1,0:T(8,128)S(1)}, f32[4,128,128]{2,1,0:T(8,128)S(1)}, u32[]{:S(2)}, u32[]{:S(2)}) %collective-permute-start.20) | collective-permute-done | bytes 262176 | tf_op jit(solution)/shard_map/ppermute | solution.py:22
  204.0 2.9 %back0.1 = (bf16[128,512]{1,0:T(8,128)(2,1)S(1)}, bf16[128,512]{1,0:T(8,128)(2,1)S(1)}, f32[128,16]{1,0:T(8,128)S(1)}) custom-call(bf16[128,2048]{1,0:T(8,128)(2,1)S(1)} %copy-done.20, bf16[128,2048]{1,0:T(8,128)(2,1)S(1)} %copy-done.23, f32[128,16]{1,0:T(8,128)S(1)} %copy-done.10, f32[128,16]{1,0:T(8,128)S(1)} %copy-done.8, f32[16,128]{1,0:T(8,128)S(1)} %bitcast.30, ...), custom_call_target="tpu_custom_call" | custom-call | flops 1207959552 | bytes 2097152 | tf_op jit(solution)/shard_map/back0/pallas_call | solution.py:402
  207.0 2.9 %back1.1 = (bf16[128,512]{1,0:T(8,128)(2,1)S(1)}, bf16[128,512]{1,0:T(8,128)(2,1)S(1)}, f32[128,16]{1,0:T(8,128)S(1)}) custom-call(bf16[128,2048]{1,0:T(8,128)(2,1)S(1)} %copy-done.20, bf16[128,2048]{1,0:T(8,128)(2,1)S(1)} %copy-done.23, f32[128,16]{1,0:T(8,128)S(1)} %copy-done.10, f32[128,16]{1,0:T(8,128)S(1)} %copy-done.8, f32[16,128]{1,0:T(8,128)S(1)} %bitcast.31, ...), custom_call_target="tpu_custom_call" | custom-call | flops 1207959552 | bytes 2097152 | tf_op jit(solution)/shard_map/back1/pallas_call | solution.py:402
  210.0 2.9 %back2.1 = (bf16[128,512]{1,0:T(8,128)(2,1)S(1)}, bf16[128,512]{1,0:T(8,128)(2,1)S(1)}, f32[128,16]{1,0:T(8,128)S(1)}) custom-call(bf16[128,2048]{1,0:T(8,128)(2,1)S(1)} %copy-done.20, bf16[128,2048]{1,0:T(8,128)(2,1)S(1)} %copy-done.23, f32[128,16]{1,0:T(8,128)S(1)} %copy-done.10, f32[128,16]{1,0:T(8,128)S(1)} %copy-done.8, f32[16,128]{1,0:T(8,128)S(1)} %bitcast.32, ...), custom_call_target="tpu_custom_call" | custom-call | flops 1207959552 | bytes 2097152 | tf_op jit(solution)/shard_map/back2/pallas_call | solution.py:402
  214.7 2.9 %back3.1 = (bf16[128,512]{1,0:T(8,128)(2,1)S(1)}, bf16[128,512]{1,0:T(8,128)(2,1)S(1)}, f32[128,16]{1,0:T(8,128)S(1)}) custom-call(bf16[128,2048]{1,0:T(8,128)(2,1)S(1)} %copy-done.20, bf16[128,2048]{1,0:T(8,128)(2,1)S(1)} %copy-done.23, f32[128,16]{1,0:T(8,128)S(1)} %copy-done.10, f32[128,16]{1,0:T(8,128)S(1)} %copy-done.8, f32[16,128]{1,0:T(8,128)S(1)} %bitcast.33, ...), custom_call_target="tpu_custom_call" | custom-call | flops 1207959552 | bytes 2097152 | tf_op jit(solution)/shard_map/back3/pallas_call | solution.py:402
  (350 shorter events, 65.4 us)
Async XLA Ops:
  10.7 55.4 %collective-permute-start = (f32[4,128,128]{2,1,0:T(8,128)S(1)}, f32[4,128,128]{2,1,0:T(8,128)S(1)}, u32[]{:S(2)}, u32[]{:S(2)}) collective-permute-start(f32[4,128,128]{2,1,0:T(8,128)S(1)} %get-tuple-element.64), channel_id=1, source_target_pairs={{0,4},{4,0},{8,12},{12,8},{16,20},{20,16},{24,28},{28,24},{1,5},{5... | collective-permute-start | bytes 786440 | tf_op jit(solution)/shard_map/ppermute | solution.py:22
  21.4 45.6 %collective-permute-start.3 = (f32[4,128,128]{2,1,0:T(8,128)S(1)}, f32[4,128,128]{2,1,0:T(8,128)S(1)}, u32[]{:S(2)}, u32[]{:S(2)}) collective-permute-start(f32[4,128,128]{2,1,0:T(8,128)S(1)} %get-tuple-element.67), channel_id=1, source_target_pairs={{0,4},{4,0},{8,12},{12,8},{16,20},{20,16},{24,28},{28,24},{1,5},{5... | collective-permute-start | bytes 786440 | tf_op jit(solution)/shard_map/ppermute | solution.py:22
  29.1 40.8 %collective-permute-start.6 = (f32[4,128,128]{2,1,0:T(8,128)S(1)}, f32[4,128,128]{2,1,0:T(8,128)S(1)}, u32[]{:S(2)}, u32[]{:S(2)}) collective-permute-start(f32[4,128,128]{2,1,0:T(8,128)S(1)} %get-tuple-element.70), channel_id=1, source_target_pairs={{0,4},{4,0},{8,12},{12,8},{16,20},{20,16},{24,28},{28,24},{1,5},{5... | collective-permute-start | bytes 786440 | tf_op jit(solution)/shard_map/ppermute | solution.py:22
  38.7 32.0 %collective-permute-start.9 = (f32[4,128,128]{2,1,0:T(8,128)S(1)}, f32[4,128,128]{2,1,0:T(8,128)S(1)}, u32[]{:S(2)}, u32[]{:S(2)}) collective-permute-start(f32[4,128,128]{2,1,0:T(8,128)S(1)} %get-tuple-element.73), channel_id=1, source_target_pairs={{0,4},{4,0},{8,12},{12,8},{16,20},{20,16},{24,28},{28,24},{1,5},{5... | collective-permute-start | bytes 786440 | tf_op jit(solution)/shard_map/ppermute | solution.py:22
  66.9 14.9 %collective-permute-start.1 = (f32[4,128,128]{2,1,0:T(8,128)S(1)}, f32[4,128,128]{2,1,0:T(8,128)S(1)}, u32[]{:S(2)}, u32[]{:S(2)}) collective-permute-start(f32[4,128,128]{2,1,0:T(8,128)S(1)} %multiply_add_fusion.35), channel_id=1, source_target_pairs={{0,8},{4,12},{8,0},{12,4},{16,24},{20,28},{24,16},{28,20},{1,9},{5... | collective-permute-start | bytes 786440 | tf_op jit(solution)/shard_map/ppermute | solution.py:22
  67.8 20.9 %collective-permute-start.4 = (f32[4,128,128]{2,1,0:T(8,128)S(1)}, f32[4,128,128]{2,1,0:T(8,128)S(1)}, u32[]{:S(2)}, u32[]{:S(2)}) collective-permute-start(f32[4,128,128]{2,1,0:T(8,128)S(1)} %multiply_add_fusion.33), channel_id=1, source_target_pairs={{0,8},{4,12},{8,0},{12,4},{16,24},{20,28},{24,16},{28,20},{1,9},{5... | collective-permute-start | bytes 786440 | tf_op jit(solution)/shard_map/ppermute | solution.py:22
  70.6 21.6 %collective-permute-start.7 = (f32[4,128,128]{2,1,0:T(8,128)S(1)}, f32[4,128,128]{2,1,0:T(8,128)S(1)}, u32[]{:S(2)}, u32[]{:S(2)}) collective-permute-start(f32[4,128,128]{2,1,0:T(8,128)S(1)} %multiply_add_fusion.31), channel_id=1, source_target_pairs={{0,8},{4,12},{8,0},{12,4},{16,24},{20,28},{24,16},{28,20},{1,9},{5... | collective-permute-start | bytes 786440 | tf_op jit(solution)/shard_map/ppermute | solution.py:22
  71.4 23.6 %collective-permute-start.10 = (f32[4,128,128]{2,1,0:T(8,128)S(1)}, f32[4,128,128]{2,1,0:T(8,128)S(1)}, u32[]{:S(2)}, u32[]{:S(2)}) collective-permute-start(f32[4,128,128]{2,1,0:T(8,128)S(1)} %multiply_add_fusion.29), channel_id=1, source_target_pairs={{0,8},{4,12},{8,0},{12,4},{16,24},{20,28},{24,16},{28,20},{1,9},{5... | collective-permute-start | bytes 786440 | tf_op jit(solution)/shard_map/ppermute | solution.py:22
  82.6 36.7 %collective-permute-start.2 = (f32[4,128,128]{2,1,0:T(8,128)S(1)}, f32[4,128,128]{2,1,0:T(8,128)S(1)}, u32[]{:S(2)}, u32[]{:S(2)}) collective-permute-start(f32[4,128,128]{2,1,0:T(8,128)S(1)} %multiply_add_fusion.34), channel_id=1, source_target_pairs={{0,16},{4,20},{8,24},{12,28},{16,0},{20,4},{24,8},{28,12},{1,17},{... | collective-permute-start | bytes 786440 | tf_op jit(solution)/shard_map/ppermute | solution.py:22
  89.4 36.9 %collective-permute-start.5 = (f32[4,128,128]{2,1,0:T(8,128)S(1)}, f32[4,128,128]{2,1,0:T(8,128)S(1)}, u32[]{:S(2)}, u32[]{:S(2)}) collective-permute-start(f32[4,128,128]{2,1,0:T(8,128)S(1)} %multiply_add_fusion.32), channel_id=1, source_target_pairs={{0,16},{4,20},{8,24},{12,28},{16,0},{20,4},{24,8},{28,12},{1,17},{... | collective-permute-start | bytes 786440 | tf_op jit(solution)/shard_map/ppermute | solution.py:22
  92.9 43.4 %collective-permute-start.8 = (f32[4,128,128]{2,1,0:T(8,128)S(1)}, f32[4,128,128]{2,1,0:T(8,128)S(1)}, u32[]{:S(2)}, u32[]{:S(2)}) collective-permute-start(f32[4,128,128]{2,1,0:T(8,128)S(1)} %multiply_add_fusion.30), channel_id=1, source_target_pairs={{0,16},{4,20},{8,24},{12,28},{16,0},{20,4},{24,8},{28,12},{1,17},{... | collective-permute-start | bytes 786440 | tf_op jit(solution)/shard_map/ppermute | solution.py:22
  95.1 52.2 %collective-permute-start.11 = (f32[4,128,128]{2,1,0:T(8,128)S(1)}, f32[4,128,128]{2,1,0:T(8,128)S(1)}, u32[]{:S(2)}, u32[]{:S(2)}) collective-permute-start(f32[4,128,128]{2,1,0:T(8,128)S(1)} %multiply_add_fusion.28), channel_id=1, source_target_pairs={{0,16},{4,20},{8,24},{12,28},{16,0},{20,4},{24,8},{28,12},{1,17},{... | collective-permute-start | bytes 786440 | tf_op jit(solution)/shard_map/ppermute | solution.py:22
  126.3 50.8 %collective-permute-start.12 = (f32[4,128,128]{2,1,0:T(8,128)}, f32[4,128,128]{2,1,0:T(8,128)}, u32[]{:S(2)}, u32[]{:S(2)}) collective-permute-start(f32[4,128,128]{2,1,0:T(8,128)} %multiply_add_fusion.26), channel_id=1, source_target_pairs={{0,16},{4,20},{8,24},{12,28},{16,0},{20,4},{24,8},{28,12},{1,17},{... | collective-permute-start | bytes 786440 | tf_op jit(solution)/shard_map/ppermute | solution.py:22
  133.5 46.9 %collective-permute-start.15 = (f32[4,128,128]{2,1,0:T(8,128)}, f32[4,128,128]{2,1,0:T(8,128)}, u32[]{:S(2)}, u32[]{:S(2)}) collective-permute-start(f32[4,128,128]{2,1,0:T(8,128)} %multiply_add_fusion.20), channel_id=1, source_target_pairs={{0,16},{4,20},{8,24},{12,28},{16,0},{20,4},{24,8},{28,12},{1,17},{... | collective-permute-start | bytes 786440 | tf_op jit(solution)/shard_map/ppermute | solution.py:22
  143.3 39.6 %collective-permute-start.18 = (f32[4,128,128]{2,1,0:T(8,128)}, f32[4,128,128]{2,1,0:T(8,128)}, u32[]{:S(2)}, u32[]{:S(2)}) collective-permute-start(f32[4,128,128]{2,1,0:T(8,128)} %multiply_add_fusion.14), channel_id=1, source_target_pairs={{0,16},{4,20},{8,24},{12,28},{16,0},{20,4},{24,8},{28,12},{1,17},{... | collective-permute-start | bytes 786440 | tf_op jit(solution)/shard_map/ppermute | solution.py:22
  153.8 32.3 %collective-permute-start.21 = (f32[4,128,128]{2,1,0:T(8,128)}, f32[4,128,128]{2,1,0:T(8,128)}, u32[]{:S(2)}, u32[]{:S(2)}) collective-permute-start(f32[4,128,128]{2,1,0:T(8,128)} %multiply_add_fusion.8), channel_id=1, source_target_pairs={{0,16},{4,20},{8,24},{12,28},{16,0},{20,4},{24,8},{28,12},{1,17},{... | collective-permute-start | bytes 786440 | tf_op jit(solution)/shard_map/ppermute | solution.py:22
  178.9 10.4 %collective-permute-start.13 = (f32[4,128,128]{2,1,0:T(8,128)S(1)}, f32[4,128,128]{2,1,0:T(8,128)S(1)}, u32[]{:S(2)}, u32[]{:S(2)}) collective-permute-start(f32[4,128,128]{2,1,0:T(8,128)S(1)} %get-tuple-element.164), channel_id=1, source_target_pairs={{0,8},{4,12},{8,0},{12,4},{16,24},{20,28},{24,16},{28,20},{1,9},{5... | collective-permute-start | bytes 786440 | tf_op jit(solution)/shard_map/ppermute | solution.py:22
  182.1 10.5 %collective-permute-start.16 = (f32[4,128,128]{2,1,0:T(8,128)S(1)}, f32[4,128,128]{2,1,0:T(8,128)S(1)}, u32[]{:S(2)}, u32[]{:S(2)}) collective-permute-start(f32[4,128,128]{2,1,0:T(8,128)S(1)} %get-tuple-element.166), channel_id=1, source_target_pairs={{0,8},{4,12},{8,0},{12,4},{16,24},{20,28},{24,16},{28,20},{1,9},{5... | collective-permute-start | bytes 786440 | tf_op jit(solution)/shard_map/ppermute | solution.py:22
  184.7 9.7 %collective-permute-start.19 = (f32[4,128,128]{2,1,0:T(8,128)S(1)}, f32[4,128,128]{2,1,0:T(8,128)S(1)}, u32[]{:S(2)}, u32[]{:S(2)}) collective-permute-start(f32[4,128,128]{2,1,0:T(8,128)S(1)} %get-tuple-element.168), channel_id=1, source_target_pairs={{0,8},{4,12},{8,0},{12,4},{16,24},{20,28},{24,16},{28,20},{1,9},{5... | collective-permute-start | bytes 786440 | tf_op jit(solution)/shard_map/ppermute | solution.py:22
  187.8 9.2 %collective-permute-start.22 = (f32[4,128,128]{2,1,0:T(8,128)S(1)}, f32[4,128,128]{2,1,0:T(8,128)S(1)}, u32[]{:S(2)}, u32[]{:S(2)}) collective-permute-start(f32[4,128,128]{2,1,0:T(8,128)S(1)} %get-tuple-element.170), channel_id=1, source_target_pairs={{0,8},{4,12},{8,0},{12,4},{16,24},{20,28},{24,16},{28,20},{1,9},{5... | collective-permute-start | bytes 786440 | tf_op jit(solution)/shard_map/ppermute | solution.py:22
  191.1 7.7 %collective-permute-start.14 = (f32[4,128,128]{2,1,0:T(8,128)S(1)}, f32[4,128,128]{2,1,0:T(8,128)S(1)}, u32[]{:S(2)}, u32[]{:S(2)}) collective-permute-start(f32[4,128,128]{2,1,0:T(8,128)S(1)} %get-tuple-element.146), channel_id=1, source_target_pairs={{0,4},{4,0},{8,12},{12,8},{16,20},{20,16},{24,28},{28,24},{1,5},{5... | collective-permute-start | bytes 786440 | tf_op jit(solution)/shard_map/ppermute | solution.py:22
  193.7 6.6 %collective-permute-start.17 = (f32[4,128,128]{2,1,0:T(8,128)S(1)}, f32[4,128,128]{2,1,0:T(8,128)S(1)}, u32[]{:S(2)}, u32[]{:S(2)}) collective-permute-start(f32[4,128,128]{2,1,0:T(8,128)S(1)} %get-tuple-element.148), channel_id=1, source_target_pairs={{0,4},{4,0},{8,12},{12,8},{16,20},{20,16},{24,28},{28,24},{1,5},{5... | collective-permute-start | bytes 786440 | tf_op jit(solution)/shard_map/ppermute | solution.py:22
  195.5 7.7 %collective-permute-start.20 = (f32[4,128,128]{2,1,0:T(8,128)S(1)}, f32[4,128,128]{2,1,0:T(8,128)S(1)}, u32[]{:S(2)}, u32[]{:S(2)}) collective-permute-start(f32[4,128,128]{2,1,0:T(8,128)S(1)} %get-tuple-element.150), channel_id=1, source_target_pairs={{0,4},{4,0},{8,12},{12,8},{16,20},{20,16},{24,28},{28,24},{1,5},{5... | collective-permute-start | bytes 786440 | tf_op jit(solution)/shard_map/ppermute | solution.py:22
  198.1 14.8 %collective-permute-start.23 = (f32[4,128,128]{2,1,0:T(8,128)S(1)}, f32[4,128,128]{2,1,0:T(8,128)S(1)}, u32[]{:S(2)}, u32[]{:S(2)}) collective-permute-start(f32[4,128,128]{2,1,0:T(8,128)S(1)} %get-tuple-element.152), channel_id=1, source_target_pairs={{0,4},{4,0},{8,12},{12,8},{16,20},{20,16},{24,28},{28,24},{1,5},{5... | collective-permute-start | bytes 786440 | tf_op jit(solution)/shard_map/ppermute | solution.py:22
  (124 other events, 852.5 us)

commit v2 on v1

--- a/solution.py
+++ b/solution.py
@@ -249,29 +249,32 @@
     step = HEADS_STEP if per % HEADS_STEP == 0 else 1
     steps = per // step
     device = lax.axis_index("ctx")
-    blocks = lax.axis_size("ctx")
 
     lower = jnp.tril(jnp.ones((rows, rows), jnp.float32))
     gates = lax.dot_general(lower, log_gate, NN, precision=topmost_level)
     gates_row = gates.T
-    totals = lax.all_gather(gates[-1], "ctx")
-    ids = jnp.arange(blocks)
     degrees = levels - 1
-
-    def group_sum(match):
-        return jnp.sum(jnp.where(match[:, None], totals, 0.0), axis=0)
+    top = degrees - 1
+    half = 2**top
+    unit = min(half, 2)
+    hops = [[(half - unit + k, half + k) for k in range(unit)]]
+    for stage in range(1, half // unit):
+        hops.append(
+            [(half + (stage - 1) * unit + k, half + stage * unit + k) for k in range(unit)]
+        )
 
     offset = jnp.zeros((heads,), jnp.float32)
+    group_total = gates[-1]
     uppers, offsets, own_sums, partner_sums = [], [], [], []
     for degree in range(degrees):
-        own = ids >> degree == device >> degree
-        other = ids >> degree == (device >> degree) ^ 1
         is_upper = device >> degree & 1 == 1
+        partner_total = from_partner(group_total, "ctx", degree)
         uppers.append(is_upper)
         offsets.append(offset)
-        own_sums.append(group_sum(own))
-        partner_sums.append(group_sum(other))
-        offset = jnp.where(is_upper, offset + partner_sums[-1], offset)
+        own_sums.append(group_total)
+        partner_sums.append(partner_total)
+        offset = jnp.where(is_upper, offset + partner_total, offset)
+        group_total = group_total + partner_total
     factors = [jnp.ones((rows, heads), jnp.float32)]
     for degree in range(degrees):
         reach = jnp.where(uppers[degree], jnp.exp(offsets[degree]), 0.0)
@@ -329,24 +332,45 @@
 
     aggregates = [state for _, _, state in prepared]
     partners = [[None] * degrees for _ in range(chunks)]
-    for degree in range(degrees):
+    for degree in range(top):
+        upper = uppers[degree]
+        own_factor = jnp.where(upper, 1.0, jnp.exp(partner_sums[degree]))
+        other_factor = jnp.where(upper, jnp.exp(own_sums[degree]), 1.0)
         for chunk in range(chunks):
             partner = from_partner(aggregates[chunk], "ctx", degree)
             partners[chunk][degree] = partner
-            upper = uppers[degree]
-            own_factor = jnp.where(upper, 1.0, jnp.exp(partner_sums[degree]))
-            other_factor = jnp.where(upper, jnp.exp(own_sums[degree]), 1.0)
             aggregates[chunk] = (
                 part_of(own_factor, chunk) * aggregates[chunk]
                 + part_of(other_factor, chunk) * partner
             )
+    for chunk in range(chunks):
+        passed = lax.ppermute(aggregates[chunk], "ctx", hops[0])
+        gathered = passed
+        for pairs in hops[1:]:
+            passed = lax.ppermute(passed, "ctx", pairs)
+            gathered = gathered + passed
+        partners[chunk][top] = gathered
 
     rows_dev = grad_final_state.shape[0]
+    own_start = device * rows_dev
+    partner_start = (device ^ half) * rows_dev
+    own_factor = jnp.where(uppers[top], 1.0, jnp.exp(partner_sums[top]))
+    other_factor = jnp.where(uppers[top], jnp.exp(own_sums[top]), 1.0)
+
+    def factor_rows(vector):
+        spread = jnp.broadcast_to(vector[:, None], (heads, size)).reshape(heads * size, 1)
+        return lax.dynamic_slice_in_dim(spread, own_start, rows_dev, 0)
+
     full_rows = jnp.concatenate(aggregates).reshape(heads * size, vsize)
-    own_rows = lax.dynamic_slice_in_dim(full_rows, device * rows_dev, rows_dev, 0)
-    seeds = lax.dynamic_update_slice_in_dim(
-        jnp.zeros((heads * size, vsize), jnp.float32), grad_final_state, device * rows_dev, 0
-    ).reshape(heads, size, vsize)
+    sent_rows = lax.dynamic_slice_in_dim(full_rows, partner_start, rows_dev, 0)
+    own_rows = factor_rows(own_factor) * lax.dynamic_slice_in_dim(
+        full_rows, own_start, rows_dev, 0
+    ) + factor_rows(other_factor) * from_partner(sent_rows, "ctx", top)
+    partner_seed = from_partner(grad_final_state, "ctx", top)
+    seeds = jnp.zeros((heads * size, vsize), jnp.float32)
+    seeds = lax.dynamic_update_slice_in_dim(seeds, grad_final_state, own_start, 0)
+    seeds = lax.dynamic_update_slice_in_dim(seeds, partner_seed, partner_start, 0)
+    seeds = own_factor[:, None, None] * seeds.reshape(heads, size, vsize)
 
     gain = norm_gain[None, :]
     finished = []
@@ -381,15 +405,25 @@
                 *partners[chunk],
             )
         )
-    grad_gain = lax.psum(sum(result[4] for result in finished)[0], "ctx")
-
-    adjoints = [seeds[chunk * per : (chunk + 1) * per] for chunk in range(chunks)]
-    for degree in reversed(range(degrees)):
+    grad_gain = sum(result[4] for result in finished)[0]
+    for degree in range(degrees):
+        grad_gain = grad_gain + from_partner(grad_gain, "ctx", degree)
+
+    adjoints = []
+    for chunk in range(chunks):
+        carried = finished[chunk][5 + top]
+        for pairs in reversed(hops[1:]):
+            back_pairs = [(target, source) for source, target in pairs]
+            carried = carried + lax.ppermute(carried, "ctx", back_pairs)
+        back_pairs = [(target, source) for source, target in hops[0]]
+        carried = lax.ppermute(carried, "ctx", back_pairs)
+        adjoints.append(seeds[chunk * per : (chunk + 1) * per] + carried)
+    for degree in reversed(range(top)):
+        upper = uppers[degree]
+        send_factor = jnp.where(upper, jnp.exp(own_sums[degree]), 1.0)
+        keep_factor = jnp.where(upper, 1.0, jnp.exp(partner_sums[degree]))
         for chunk in range(chunks):
             adjoint = adjoints[chunk]
-            upper = uppers[degree]
-            send_factor = jnp.where(upper, jnp.exp(own_sums[degree]), 1.0)
-            keep_factor = jnp.where(upper, 1.0, jnp.exp(partner_sums[degree]))
             outgoing = finished[chunk][5 + degree] + part_of(send_factor, chunk) * adjoint
             incoming = from_partner(outgoing, "ctx", degree)
             adjoints[chunk] = part_of(keep_factor, chunk) * adjoint + incoming

time: 221 us -> 192 us (0.87)
  starting transfers between devices: 22.4 us -> 69.3 us
  blocking collectives: 40 us -> 0 us
  waiting for transfers between devices: 50.1 us -> 34.5 us
  local copies, waits for them, and re-layouts: 31.2 us -> 19.3 us
  other arithmetic: 18.3 us -> 9.92 us
    ppermute x24, starting transfers between devices: 22.4 us -> 57.8 us  [from_partner(): return lax.ppermute(value, axis, pairs)]
    all_gather x1 -> x0, blocking collectives: 21.4 us -> none  [local(): totals = lax.all_gather(gates[-1], 'ctx')]
    psum x1 -> x0, blocking collectives: 18.7 us -> none  [local(): grad_gain = lax.psum(sum((result[4] for result in finished))[0], 'ctx')]
    ppermute x24, waiting for transfers between devices: 50.1 us -> 34.5 us  [from_partner(): return lax.ppermute(value, axis, pairs)]
    ppermute x0 -> x16, starting transfers between devices: none -> 11.6 us  [the longest x4 3.27 us: local(): carried = carried + lax.ppermute(carried, 'ctx', back_pairs)]
    unnamed x250 -> x168, local copies, waits for them, and re-layouts: 24.7 us -> 15.7 us
    add x8 -> x3, other arithmetic: 7.55 us -> 2.94 us  [local(): finished[chunk][5 + degree] + part_of(send_factor, chunk) * adjoint]
    add x12 -> x8, other arithmetic: 5.32 us -> 0.8 us  [local(): part_of(own_factor, chunk) * aggregates[chunk]]
  transfers between devices with their start and end apart: 24 -> 40, of which waited for: 8 -> 12; matrix products, arithmetic and copies ran while one was open for 10% -> 6% of each run, Pallas kernels for 21% -> 28%
where the time goes in v2:
time: 192 us; the launch traced here: 191 us
  starting transfers between devices  69.3 us (36%)
  Pallas kernels  55.8 us (29%)
  waiting for transfers between devices  34.5 us (18%)
  local copies, waits for them, and re-layouts  19.3 us (10%)
  other arithmetic  9.92 us (5%)
    ppermute x24, starting transfers between devices, from_partner(): return lax.ppermute(value, axis, pairs)  57.8 us
    ppermute x24, waiting for transfers between devices, from_partner(): return lax.ppermute(value, axis, pairs)  34.5 us
    pallas_call x4, Pallas kernels, local(): call(functools.partial(prepare_kernel, chunk * per), f'prepare{chunk}', [...  24.8 us
    pallas_call x4, Pallas kernels, local(): call(functools.partial(finish_kernel, chunk * per, levels), f'finish{chun...  19.4 us
    unnamed x168, local copies, waits for them, and re-layouts  15.7 us
    pallas_call x4, Pallas kernels, local(): call(functools.partial(back_kernel, chunk * per), f'back{chunk}', [wide(c...  11.6 us
  transfers between devices with their start and end apart: 40, of which 12 were waited for; matrix products, arithmetic and copies ran while one was open for 6% of the time, Pallas kernels for 28%

profile of v2, /device:TPU:0, one launch (start us, length us, event | category | flops | bytes accessed | tf_op | source)
XLA Modules:
  0.0 190.9 jit_solution(5908788048413814037)
XLA Ops:
  1.8 3.0 %collective-permute-start = (f32[16]{0:T(128)S(1)}, f32[16]{0:T(128)S(1)}, u32[]{:S(2)}, u32[]{:S(2)}) collective-permute-start(f32[16]{0:T(128)S(1)} %slice_reduce_fusion), channel_id=1, source_target_pairs={{0,4},{4,0},{8,12},{12,8},{16,20},{20,16},{24,28},{28,24},{1,5},{5... | collective-permute-start | bytes 200 | tf_op jit(solution)/shard_map/ppermute | solution.py:22
  4.8 2.6 %collective-permute-start.19 = (f32[256,128]{1,0:T(8,128)}, f32[256,128]{1,0:T(8,128)}, u32[]{:S(2)}, u32[]{:S(2)}) collective-permute-start(f32[256,128]{1,0:T(8,128)} %param.17), channel_id=1, source_target_pairs={{0,16},{4,20},{8,24},{12,28},{16,0},{20,4},{24,8},{28,12},{1,17},{... | collective-permute-start | bytes 393224 | tf_op jit(solution)/shard_map/ppermute | solution.py:22
  9.6 6.2 %prepare3.1 = (f32[4,128,128]{2,1,0:T(8,128)S(1)}, f32[4,128,128]{2,1,0:T(8,128)S(1)}, f32[4,128,128]{2,1,0:T(8,128)S(1)}) custom-call(bf16[128,2048]{1,0:T(8,128)(2,1)S(1)} %copy-done.3, bf16[128,2048]{1,0:T(8,128)(2,1)S(1)} %copy-done.5, f32[128,16]{1,0:T(8,128)S(1)} %copy.41.beta_ref, f32[128,16]{1,0:T(8,128)S(1)} %copy.42.cc_ref, f32[16,128]{1,0:T(8,128)S(1)} %bitcast.21), custom_call_target="tpu_custom_call" | custom-call | flops 3221225472 | bytes 2097152 | tf_op jit(solution)/shard_map/prepare3/pallas_call | solution.py:320
  17.8 6.2 %prepare2.1 = (f32[4,128,128]{2,1,0:T(8,128)S(1)}, f32[4,128,128]{2,1,0:T(8,128)S(1)}, f32[4,128,128]{2,1,0:T(8,128)S(1)}) custom-call(bf16[128,2048]{1,0:T(8,128)(2,1)S(1)} %copy-done.3, bf16[128,2048]{1,0:T(8,128)(2,1)S(1)} %copy-done.5, f32[128,16]{1,0:T(8,128)S(1)} %copy.41.beta_ref, f32[128,16]{1,0:T(8,128)S(1)} %copy.42.cc_ref, f32[16,128]{1,0:T(8,128)S(1)} %bitcast.22), custom_call_target="tpu_custom_call" | custom-call | flops 3221225472 | bytes 2097152 | tf_op jit(solution)/shard_map/prepare2/pallas_call | solution.py:320
  26.2 6.2 %prepare1.1 = (f32[4,128,128]{2,1,0:T(8,128)S(1)}, f32[4,128,128]{2,1,0:T(8,128)S(1)}, f32[4,128,128]{2,1,0:T(8,128)S(1)}) custom-call(bf16[128,2048]{1,0:T(8,128)(2,1)S(1)} %copy-done.3, bf16[128,2048]{1,0:T(8,128)(2,1)S(1)} %copy-done.5, f32[128,16]{1,0:T(8,128)S(1)} %copy.41.beta_ref, f32[128,16]{1,0:T(8,128)S(1)} %copy.42.cc_ref, f32[16,128]{1,0:T(8,128)S(1)} %bitcast.23), custom_call_target="tpu_custom_call" | custom-call | flops 3221225472 | bytes 2097152 | tf_op jit(solution)/shard_map/prepare1/pallas_call | solution.py:320
  34.4 6.2 %prepare0.1 = (f32[4,128,128]{2,1,0:T(8,128)S(1)}, f32[4,128,128]{2,1,0:T(8,128)S(1)}, f32[4,128,128]{2,1,0:T(8,128)S(1)}) custom-call(bf16[128,2048]{1,0:T(8,128)(2,1)S(1)} %copy-done.4, bf16[128,2048]{1,0:T(8,128)(2,1)S(1)} %copy-done.6, f32[128,16]{1,0:T(8,128)S(1)} %copy.41.beta_ref, f32[128,16]{1,0:T(8,128)S(1)} %copy.42.cc_ref, f32[16,128]{1,0:T(8,128)S(1)} %bitcast.24), custom_call_target="tpu_custom_call" | custom-call | flops 3221225472 | bytes 2097152 | tf_op jit(solution)/shard_map/prepare0/pallas_call | solution.py:320
  54.1 3.9 %collective-permute-done.15.refs_1_ = f32[4,128,128]{2,1,0:T(8,128)S(1)} collective-permute-done((f32[4,128,128]{2,1,0:T(8,128)S(1)}, f32[4,128,128]{2,1,0:T(8,128)S(1)}, u32[]{:S(2)}, u32[]{:S(2)}) %collective-permute-start.15) | collective-permute-done | bytes 262176 | tf_op jit(solution)/shard_map/ppermute | solution.py:22
  59.7 3.9 %collective-permute-done.11.refs_1_ = f32[4,128,128]{2,1,0:T(8,128)S(1)} collective-permute-done((f32[4,128,128]{2,1,0:T(8,128)S(1)}, f32[4,128,128]{2,1,0:T(8,128)S(1)}, u32[]{:S(2)}, u32[]{:S(2)}) %collective-permute-start.11) | collective-permute-done | bytes 262176 | tf_op jit(solution)/shard_map/ppermute | solution.py:22
  64.4 3.5 %collective-permute-done.7.refs_1_ = f32[4,128,128]{2,1,0:T(8,128)S(1)} collective-permute-done((f32[4,128,128]{2,1,0:T(8,128)S(1)}, f32[4,128,128]{2,1,0:T(8,128)S(1)}, u32[]{:S(2)}, u32[]{:S(2)}) %collective-permute-start.7) | collective-permute-done | bytes 262176 | tf_op jit(solution)/shard_map/ppermute | solution.py:22
  76.9 4.9 %finish3.1 = (bf16[128,512]{1,0:T(8,128)(2,1)S(1)}, f32[4,128,128]{2,1,0:T(8,128)S(1)}, f32[4,128,128]{2,1,0:T(8,128)S(1)}, f32[128,64]{1,0:T(8,128)S(1)}, f32[1...) custom-call(bf16[128,2048]{1,0:T(8,128)(2,1)S(1)} %copy-done.1, ...), custom_call_target="tpu_custom_call" | custom-call | flops 3019898880 | bytes 2097152 | tf_op jit(solution)/shard_map/finish3/pallas_call | solution.py:380
  82.9 4.9 %finish2.1 = (bf16[128,512]{1,0:T(8,128)(2,1)S(1)}, f32[4,128,128]{2,1,0:T(8,128)S(1)}, f32[4,128,128]{2,1,0:T(8,128)S(1)}, f32[128,64]{1,0:T(8,128)S(1)}, f32[1...) custom-call(bf16[128,2048]{1,0:T(8,128)(2,1)S(1)} %copy-done.1, ...), custom_call_target="tpu_custom_call" | custom-call | flops 3019898880 | bytes 2097152 | tf_op jit(solution)/shard_map/finish2/pallas_call | solution.py:380
  89.6 4.9 %finish0.1 = (bf16[128,512]{1,0:T(8,128)(2,1)S(1)}, f32[4,128,128]{2,1,0:T(8,128)S(1)}, f32[4,128,128]{2,1,0:T(8,128)S(1)}, f32[128,64]{1,0:T(8,128)S(1)}, f32[1...) custom-call(bf16[128,2048]{1,0:T(8,128)(2,1)S(1)} %copy-done.1, ...), custom_call_target="tpu_custom_call" | custom-call | flops 3019898880 | bytes 2097152 | tf_op jit(solution)/shard_map/finish0/pallas_call | solution.py:380
  95.6 4.9 %finish1.1 = (bf16[128,512]{1,0:T(8,128)(2,1)S(1)}, f32[4,128,128]{2,1,0:T(8,128)S(1)}, f32[4,128,128]{2,1,0:T(8,128)S(1)}, f32[128,64]{1,0:T(8,128)S(1)}, f32[1...) custom-call(bf16[128,2048]{1,0:T(8,128)(2,1)S(1)} %copy-done.1, ...), custom_call_target="tpu_custom_call" | custom-call | flops 3019898880 | bytes 2097152 | tf_op jit(solution)/shard_map/finish1/pallas_call | solution.py:380
  102.2 18.5 %collective-permute-start.39 = (f32[256,128]{1,0:T(8,128)S(1)}, f32[256,128]{1,0:T(8,128)S(1)}, u32[]{:S(2)}, u32[]{:S(2)}) collective-permute-start(f32[256,128]{1,0:T(8,128)S(1)} %constant_dynamic-slice_fusion), channel_id=1, source_target_pairs={{0,16},{4,20},{8,24},{12,28},{16,0},{20,4},{24,8},{28,12},{1,17},{... | collective-permute-start | bytes 393224 | tf_op jit(solution)/shard_map/ppermute | solution.py:22
  123.3 6.4 %collective-permute-start.22 = (f32[4,128,128]{2,1,0:T(8,128)S(1)}, f32[4,128,128]{2,1,0:T(8,128)S(1)}, u32[]{:S(2)}, u32[]{:S(2)}) collective-permute-start(f32[4,128,128]{2,1,0:T(8,128)S(1)} %multiply_add_fusion.14), channel_id=1, source_target_pairs={{0,8},{4,12},{8,0},{12,4},{16,24},{20,28},{24,16},{28,20},{1,9},{5... | collective-permute-start | bytes 786440 | tf_op jit(solution)/shard_map/ppermute | solution.py:22
  133.1 2.2 %collective-permute-done.36 = f32[128]{0:T(128)S(1)} collective-permute-done((f32[128]{0:T(128)S(1)}, f32[128]{0:T(128)S(1)}, u32[]{:S(2)}, u32[]{:S(2)}) %collective-permute-start.36) | collective-permute-done | bytes 544 | tf_op jit(solution)/shard_map/ppermute | solution.py:22
  137.4 9.1 %collective-permute-start.34 = (f32[4,128,128]{2,1,0:T(8,128)}, f32[4,128,128]{2,1,0:T(8,128)}, u32[]{:S(2)}, u32[]{:S(2)}) collective-permute-start(f32[4,128,128]{2,1,0:T(8,128)} %get-tuple-element.145), channel_id=1, source_target_pairs={{0,8},{4,12},{8,0},{12,4},{16,24},{20,28},{24,16},{28,20},{1,9},{5... | collective-permute-start | bytes 786440 | tf_op jit(solution)/shard_map/ppermute | solution.py:22
  152.1 7.2 %collective-permute-done.38 = f32[128]{0:T(128)} collective-permute-done((f32[128]{0:T(128)}, f32[128]{0:T(128)}, u32[]{:S(2)}, u32[]{:S(2)}) %collective-permute-start.38) | collective-permute-done | bytes 544 | tf_op jit(solution)/shard_map/ppermute | solution.py:22
  166.9 3.0 %collective-permute-done.23 = f32[4,128,128]{2,1,0:T(8,128)S(1)} collective-permute-done((f32[4,128,128]{2,1,0:T(8,128)}, f32[4,128,128]{2,1,0:T(8,128)S(1)}, u32[]{:S(2)}, u32[]{:S(2)}) %collective-permute-start.23) | collective-permute-done | bytes 262176 | tf_op jit(solution)/shard_map/ppermute | solution.py:22
  171.0 2.9 %back0.1 = (bf16[128,512]{1,0:T(8,128)(2,1)S(1)}, bf16[128,512]{1,0:T(8,128)(2,1)S(1)}, f32[128,16]{1,0:T(8,128)S(1)}) custom-call(bf16[128,2048]{1,0:T(8,128)(2,1)S(1)} %copy-done.4, bf16[128,2048]{1,0:T(8,128)(2,1)S(1)} %copy-done.6, f32[128,16]{1,0:T(8,128)S(1)} %copy.41.beta_ref, f32[128,16]{1,0:T(8,128)S(1)} %copy.42.cc_ref, f32[16,128]{1,0:T(8,128)S(1)} %bitcast.29, ...), custom_call_target="tpu_custom_call" | custom-call | flops 1207959552 | bytes 2097152 | tf_op jit(solution)/shard_map/back0/pallas_call | solution.py:436
  174.8 2.7 %collective-permute-done.35 = f32[4,128,128]{2,1,0:T(8,128)S(1)} collective-permute-done((f32[4,128,128]{2,1,0:T(8,128)S(1)}, f32[4,128,128]{2,1,0:T(8,128)S(1)}, u32[]{:S(2)}, u32[]{:S(2)}) %collective-permute-start.35) | collective-permute-done | bytes 262176 | tf_op jit(solution)/shard_map/ppermute | solution.py:22
  178.6 2.9 %back1.1 = (bf16[128,512]{1,0:T(8,128)(2,1)S(1)}, bf16[128,512]{1,0:T(8,128)(2,1)S(1)}, f32[128,16]{1,0:T(8,128)S(1)}) custom-call(bf16[128,2048]{1,0:T(8,128)(2,1)S(1)} %copy-done.4, bf16[128,2048]{1,0:T(8,128)(2,1)S(1)} %copy-done.6, f32[128,16]{1,0:T(8,128)S(1)} %copy.41.beta_ref, f32[128,16]{1,0:T(8,128)S(1)} %copy.42.cc_ref, f32[16,128]{1,0:T(8,128)S(1)} %bitcast.30, ...), custom_call_target="tpu_custom_call" | custom-call | flops 1207959552 | bytes 2097152 | tf_op jit(solution)/shard_map/back1/pallas_call | solution.py:436
  181.5 2.9 %back3.1 = (bf16[128,512]{1,0:T(8,128)(2,1)S(1)}, bf16[128,512]{1,0:T(8,128)(2,1)S(1)}, f32[128,16]{1,0:T(8,128)S(1)}) custom-call(bf16[128,2048]{1,0:T(8,128)(2,1)S(1)} %copy-done.4, bf16[128,2048]{1,0:T(8,128)(2,1)S(1)} %copy-done.6, f32[128,16]{1,0:T(8,128)S(1)} %copy.41.beta_ref, f32[128,16]{1,0:T(8,128)S(1)} %copy.42.cc_ref, f32[16,128]{1,0:T(8,128)S(1)} %bitcast.31, ...), custom_call_target="tpu_custom_call" | custom-call | flops 1207959552 | bytes 2097152 | tf_op jit(solution)/shard_map/back3/pallas_call | solution.py:436
  186.2 2.9 %back2.1 = (bf16[128,512]{1,0:T(8,128)(2,1)S(1)}, bf16[128,512]{1,0:T(8,128)(2,1)S(1)}, f32[128,16]{1,0:T(8,128)S(1)}) custom-call(bf16[128,2048]{1,0:T(8,128)(2,1)S(1)} %copy-done.4, bf16[128,2048]{1,0:T(8,128)(2,1)S(1)} %copy-done.6, f32[128,16]{1,0:T(8,128)S(1)} %copy.41.beta_ref, f32[128,16]{1,0:T(8,128)S(1)} %copy.42.cc_ref, f32[16,128]{1,0:T(8,128)S(1)} %bitcast.32, ...), custom_call_target="tpu_custom_call" | custom-call | flops 1207959552 | bytes 2097152 | tf_op jit(solution)/shard_map/back2/pallas_call | solution.py:436
  (295 shorter events, 67.2 us)
Async XLA Ops:
  1.8 40.6 %collective-permute-start = (f32[16]{0:T(128)S(1)}, f32[16]{0:T(128)S(1)}, u32[]{:S(2)}, u32[]{:S(2)}) collective-permute-start(f32[16]{0:T(128)S(1)} %slice_reduce_fusion), channel_id=1, source_target_pairs={{0,4},{4,0},{8,12},{12,8},{16,20},{20,16},{24,28},{28,24},{1,5},{5... | collective-permute-start | bytes 200 | tf_op jit(solution)/shard_map/ppermute | solution.py:22
  4.8 68.3 %collective-permute-start.19 = (f32[256,128]{1,0:T(8,128)}, f32[256,128]{1,0:T(8,128)}, u32[]{:S(2)}, u32[]{:S(2)}) collective-permute-start(f32[256,128]{1,0:T(8,128)} %param.17), channel_id=1, source_target_pairs={{0,16},{4,20},{8,24},{12,28},{16,0},{20,4},{24,8},{28,12},{1,17},{... | collective-permute-start | bytes 393224 | tf_op jit(solution)/shard_map/ppermute | solution.py:22
  17.2 30.9 %collective-permute-start.14 = (f32[4,128,128]{2,1,0:T(8,128)S(1)}, f32[4,128,128]{2,1,0:T(8,128)S(1)}, u32[]{:S(2)}, u32[]{:S(2)}) collective-permute-start(f32[4,128,128]{2,1,0:T(8,128)S(1)} %get-tuple-element.73), channel_id=1, source_target_pairs={{0,4},{4,0},{8,12},{12,8},{16,20},{20,16},{24,28},{28,24},{1,5},{5... | collective-permute-start | bytes 786440 | tf_op jit(solution)/shard_map/ppermute | solution.py:22
  24.7 23.9 %collective-permute-start.10 = (f32[4,128,128]{2,1,0:T(8,128)S(1)}, f32[4,128,128]{2,1,0:T(8,128)S(1)}, u32[]{:S(2)}, u32[]{:S(2)}) collective-permute-start(f32[4,128,128]{2,1,0:T(8,128)S(1)} %get-tuple-element.70), channel_id=1, source_target_pairs={{0,4},{4,0},{8,12},{12,8},{16,20},{20,16},{24,28},{28,24},{1,5},{5... | collective-permute-start | bytes 786440 | tf_op jit(solution)/shard_map/ppermute | solution.py:22
  33.8 16.6 %collective-permute-start.6 = (f32[4,128,128]{2,1,0:T(8,128)S(1)}, f32[4,128,128]{2,1,0:T(8,128)S(1)}, u32[]{:S(2)}, u32[]{:S(2)}) collective-permute-start(f32[4,128,128]{2,1,0:T(8,128)S(1)} %get-tuple-element.67), channel_id=1, source_target_pairs={{0,4},{4,0},{8,12},{12,8},{16,20},{20,16},{24,28},{28,24},{1,5},{5... | collective-permute-start | bytes 786440 | tf_op jit(solution)/shard_map/ppermute | solution.py:22
  48.1 23.4 %collective-permute-start.18 = (f32[16]{0:T(128)S(1)}, f32[16]{0:T(128)S(1)}, u32[]{:S(2)}, u32[]{:S(2)}) collective-permute-start(f32[16]{0:T(128)S(1)} %get-tuple-element.134), channel_id=1, source_target_pairs={{0,16},{4,20},{8,24},{12,28},{16,0},{20,4},{24,8},{28,12},{1,17},{... | collective-permute-start | bytes 200 | tf_op jit(solution)/shard_map/ppermute | solution.py:22
  50.4 13.2 %collective-permute-start.11 = (f32[4,128,128]{2,1,0:T(8,128)S(1)}, f32[4,128,128]{2,1,0:T(8,128)S(1)}, u32[]{:S(2)}, u32[]{:S(2)}) collective-permute-start(f32[4,128,128]{2,1,0:T(8,128)S(1)} %multiply_add_fusion.19), channel_id=1, source_target_pairs={{0,8},{4,12},{8,0},{12,4},{16,24},{20,28},{24,16},{28,20},{1,9},{5... | collective-permute-start | bytes 786440 | tf_op jit(solution)/shard_map/ppermute | solution.py:22
  52.4 15.5 %collective-permute-start.7 = (f32[4,128,128]{2,1,0:T(8,128)S(1)}, f32[4,128,128]{2,1,0:T(8,128)S(1)}, u32[]{:S(2)}, u32[]{:S(2)}) collective-permute-start(f32[4,128,128]{2,1,0:T(8,128)S(1)} %multiply_add_fusion.21), channel_id=1, source_target_pairs={{0,8},{4,12},{8,0},{12,4},{16,24},{20,28},{24,16},{28,20},{1,9},{5... | collective-permute-start | bytes 786440 | tf_op jit(solution)/shard_map/ppermute | solution.py:22
  58.0 12.7 %collective-permute-start.3 = (f32[4,128,128]{2,1,0:T(8,128)S(1)}, f32[4,128,128]{2,1,0:T(8,128)S(1)}, u32[]{:S(2)}, u32[]{:S(2)}) collective-permute-start(f32[4,128,128]{2,1,0:T(8,128)S(1)} %multiply_add_fusion.23), channel_id=1, source_target_pairs={{0,8},{4,12},{8,0},{12,4},{16,24},{20,28},{24,16},{28,20},{1,9},{5... | collective-permute-start | bytes 786440 | tf_op jit(solution)/shard_map/ppermute | solution.py:22
  74.8 20.5 %collective-permute-start.9 = (f32[4,128,128]{2,1,0:T(8,128)S(1)}, f32[4,128,128]{2,1,0:T(8,128)S(1)}, u32[]{:S(2)}, u32[]{:S(2)}) collective-permute-start(f32[4,128,128]{2,1,0:T(8,128)S(1)} %collective-permute-done.8), channel_id=1, source_target_pairs={{16,24},{20,28},{17,25},{21,29},{18,26},{22,30},{19,27},{23,31}} | collective-permute-start | bytes 786440 | tf_op jit(solution)/shard_map/ppermute | solution.py:350
  75.5 13.8 %collective-permute-start.5 = (f32[4,128,128]{2,1,0:T(8,128)S(1)}, f32[4,128,128]{2,1,0:T(8,128)S(1)}, u32[]{:S(2)}, u32[]{:S(2)}) collective-permute-start(f32[4,128,128]{2,1,0:T(8,128)S(1)} %collective-permute-done.4), channel_id=1, source_target_pairs={{16,24},{20,28},{17,25},{21,29},{18,26},{22,30},{19,27},{23,31}} | collective-permute-start | bytes 786440 | tf_op jit(solution)/shard_map/ppermute | solution.py:350
  81.8 38.9 %collective-permute-start.32 = (f32[4,128,128]{2,1,0:T(8,128)S(1)}, f32[4,128,128]{2,1,0:T(8,128)S(1)}, u32[]{:S(2)}, u32[]{:S(2)}) collective-permute-start(f32[4,128,128]{2,1,0:T(8,128)S(1)} %get-tuple-element.99), channel_id=1, source_target_pairs={{24,16},{28,20},{25,17},{29,21},{26,18},{30,22},{27,19},{31,23}} | collective-permute-start | bytes 786440 | tf_op jit(solution)/shard_map/ppermute | solution.py:417
  88.5 33.0 %collective-permute-start.28 = (f32[4,128,128]{2,1,0:T(8,128)S(1)}, f32[4,128,128]{2,1,0:T(8,128)S(1)}, u32[]{:S(2)}, u32[]{:S(2)}) collective-permute-start(f32[4,128,128]{2,1,0:T(8,128)S(1)} %get-tuple-element.92), channel_id=1, source_target_pairs={{24,16},{28,20},{25,17},{29,21},{26,18},{30,22},{27,19},{31,23}} | collective-permute-start | bytes 786440 | tf_op jit(solution)/shard_map/ppermute | solution.py:417
  100.5 21.7 %collective-permute-start.24 = (f32[4,128,128]{2,1,0:T(8,128)S(1)}, f32[4,128,128]{2,1,0:T(8,128)S(1)}, u32[]{:S(2)}, u32[]{:S(2)}) collective-permute-start(f32[4,128,128]{2,1,0:T(8,128)S(1)} %get-tuple-element.85), channel_id=1, source_target_pairs={{24,16},{28,20},{25,17},{29,21},{26,18},{30,22},{27,19},{31,23}} | collective-permute-start | bytes 786440 | tf_op jit(solution)/shard_map/ppermute | solution.py:417
  101.3 21.9 %collective-permute-start.21 = (f32[4,128,128]{2,1,0:T(8,128)S(1)}, f32[4,128,128]{2,1,0:T(8,128)S(1)}, u32[]{:S(2)}, u32[]{:S(2)}) collective-permute-start(f32[4,128,128]{2,1,0:T(8,128)S(1)} %add.183), channel_id=1, source_target_pairs={{16,8},{20,12},{17,9},{21,13},{18,10},{22,14},{19,11},{23,15}} | collective-permute-start | bytes 786440 | tf_op jit(solution)/shard_map/ppermute | solution.py:419
  102.2 29.6 %collective-permute-start.39 = (f32[256,128]{1,0:T(8,128)S(1)}, f32[256,128]{1,0:T(8,128)S(1)}, u32[]{:S(2)}, u32[]{:S(2)}) collective-permute-start(f32[256,128]{1,0:T(8,128)S(1)} %constant_dynamic-slice_fusion), channel_id=1, source_target_pairs={{0,16},{4,20},{8,24},{12,28},{16,0},{20,4},{24,8},{28,12},{1,17},{... | collective-permute-start | bytes 393224 | tf_op jit(solution)/shard_map/ppermute | solution.py:22
  120.8 14.6 %collective-permute-start.33 = (f32[4,128,128]{2,1,0:T(8,128)S(1)}, f32[4,128,128]{2,1,0:T(8,128)S(1)}, u32[]{:S(2)}, u32[]{:S(2)}) collective-permute-start(f32[4,128,128]{2,1,0:T(8,128)S(1)} %add.201), channel_id=1, source_target_pairs={{16,8},{20,12},{17,9},{21,13},{18,10},{22,14},{19,11},{23,15}} | collective-permute-start | bytes 786440 | tf_op jit(solution)/shard_map/ppermute | solution.py:419
  121.5 13.8 %collective-permute-start.29 = (f32[4,128,128]{2,1,0:T(8,128)S(1)}, f32[4,128,128]{2,1,0:T(8,128)S(1)}, u32[]{:S(2)}, u32[]{:S(2)}) collective-permute-start(f32[4,128,128]{2,1,0:T(8,128)S(1)} %add.195), channel_id=1, source_target_pairs={{16,8},{20,12},{17,9},{21,13},{18,10},{22,14},{19,11},{23,15}} | collective-permute-start | bytes 786440 | tf_op jit(solution)/shard_map/ppermute | solution.py:419
  122.3 13.1 %collective-permute-start.25 = (f32[4,128,128]{2,1,0:T(8,128)S(1)}, f32[4,128,128]{2,1,0:T(8,128)S(1)}, u32[]{:S(2)}, u32[]{:S(2)}) collective-permute-start(f32[4,128,128]{2,1,0:T(8,128)S(1)} %add.189), channel_id=1, source_target_pairs={{16,8},{20,12},{17,9},{21,13},{18,10},{22,14},{19,11},{23,15}} | collective-permute-start | bytes 786440 | tf_op jit(solution)/shard_map/ppermute | solution.py:419
  135.3 14.1 %collective-permute-start.37 = (f32[128]{0:T(128)S(1)}, f32[128]{0:T(128)S(1)}, u32[]{:S(2)}, u32[]{:S(2)}) collective-permute-start(f32[128]{0:T(128)S(1)} %add.216), channel_id=1, source_target_pairs={{0,8},{4,12},{8,0},{12,4},{16,24},{20,28},{24,16},{28,20},{1,9},{5... | collective-permute-start | bytes 1544 | tf_op jit(solution)/shard_map/ppermute | solution.py:22
  137.4 23.6 %collective-permute-start.34 = (f32[4,128,128]{2,1,0:T(8,128)}, f32[4,128,128]{2,1,0:T(8,128)}, u32[]{:S(2)}, u32[]{:S(2)}) collective-permute-start(f32[4,128,128]{2,1,0:T(8,128)} %get-tuple-element.145), channel_id=1, source_target_pairs={{0,8},{4,12},{8,0},{12,4},{16,24},{20,28},{24,16},{28,20},{1,9},{5... | collective-permute-start | bytes 786440 | tf_op jit(solution)/shard_map/ppermute | solution.py:22
  146.5 14.5 %collective-permute-start.30 = (f32[4,128,128]{2,1,0:T(8,128)}, f32[4,128,128]{2,1,0:T(8,128)}, u32[]{:S(2)}, u32[]{:S(2)}) collective-permute-start(f32[4,128,128]{2,1,0:T(8,128)} %get-tuple-element.146), channel_id=1, source_target_pairs={{0,8},{4,12},{8,0},{12,4},{16,24},{20,28},{24,16},{28,20},{1,9},{5... | collective-permute-start | bytes 786440 | tf_op jit(solution)/shard_map/ppermute | solution.py:22
  146.6 14.4 %collective-permute-start.26 = (f32[4,128,128]{2,1,0:T(8,128)}, f32[4,128,128]{2,1,0:T(8,128)}, u32[]{:S(2)}, u32[]{:S(2)}) collective-permute-start(f32[4,128,128]{2,1,0:T(8,128)} %get-tuple-element.147), channel_id=1, source_target_pairs={{0,8},{4,12},{8,0},{12,4},{16,24},{20,28},{24,16},{28,20},{1,9},{5... | collective-permute-start | bytes 786440 | tf_op jit(solution)/shard_map/ppermute | solution.py:22
  165.4 19.1 %collective-permute-start.31 = (f32[4,128,128]{2,1,0:T(8,128)S(1)}, f32[4,128,128]{2,1,0:T(8,128)S(1)}, u32[]{:S(2)}, u32[]{:S(2)}) collective-permute-start(f32[4,128,128]{2,1,0:T(8,128)S(1)} %get-tuple-element.150), channel_id=1, source_target_pairs={{0,4},{4,0},{8,12},{12,8},{16,20},{20,16},{24,28},{28,24},{1,5},{5... | collective-permute-start | bytes 786440 | tf_op jit(solution)/shard_map/ppermute | solution.py:22
  (99 other events, 494.7 us)
